TPU v7x, 32 devices: a whole 2x2x4 slice. The times are simulated.
32 devices in a mesh: expert: 8 (over z, x), dp: 4 (over y, core).
Axes of the slice: x: 2, y: 2, z: 4, core: 2. Of those that a mesh axis runs over, the one named last changes fastest.
Arguments:
- tokens: bfloat16 [32, 1024, 512], P(('expert', 'dp')), may hold values from -6 to 6
- segment_ids: int32 [32, 1024], P(('expert', 'dp')), may hold values from 0 to 7, never falling along the last dimension, each value on 1 to 512 neighbouring positions
- live_tokens: int32 [32], P(('expert', 'dp')), may hold values from 1 to 1024, 16384 in all
- cotangent: bfloat16 [32, 1024, 512], P(('expert', 'dp')), may hold values from -6 to 6
- ln1_gain: bfloat16 [512], replicated, may hold values from 0.5 to 1.5
- ln1_bias: bfloat16 [512], replicated, may hold values from -2 to 2
- qkv_weight: bfloat16 [512, 1536], replicated, may hold values from -0.25 to 0.25
- attn_weight: bfloat16 [512, 512], replicated, may hold values from -0.75 to 0.75
- ln2_gain: bfloat16 [512], replicated, may hold values from 0.5 to 1.5
- ln2_bias: bfloat16 [512], replicated, may hold values from -2 to 2
- task_logits: float32 [8, 2], P('expert'), may hold values from -3 to 3
- expert_in: bfloat16 [8, 512, 1024], P('expert'), may hold values from -0.25 to 0.25
- expert_out: bfloat16 [8, 1024, 512], P('expert'), may hold values from -0.125 to 0.125
Outputs:
- layer_out: bfloat16 [32, 1024, 512], P(('expert', 'dp'))
- input_grad: bfloat16 [32, 1024, 512], P(('expert', 'dp'))
- ln1_gain_grad: float32 [512], replicated
- ln1_bias_grad: float32 [512], replicated
- qkv_grad: float32 [512, 1536], replicated
- attn_grad: float32 [512, 512], replicated
- ln2_gain_grad: float32 [512], replicated
- ln2_bias_grad: float32 [512], replicated
- logits_grad: float32 [8, 2], P('expert')
- expert_in_grad: float32 [8, 512, 1024], P('expert')
- expert_out_grad: float32 [8, 1024, 512], P('expert')
Inputs may be any that keep to these rules, and one draw needn't show every extreme that they name: `segment_ids`: within each packed row, segment ids never fall; each sentence has 1 to 512 tokens. `live_tokens`: the live counts of all rows sum to 16384; some row is wholly live.
All inputs are finite; a program needn't handle non-finite values. No bound on the sum of `live_tokens` on one device may be relied on, other than what follows from the above.
Results may differ from a plain program's by a relative error of at most 0.01.
Values may be sent and summed in bfloat16 or wider, within the bound.
A program may use at most 192 MiB of HBM per device.

v0:
```python
import functools

import jax
import jax.numpy as jnp
from jax import lax
from jax.experimental import pallas as pl
from jax.experimental.pallas import tpu as pltpu
from jax.sharding import PartitionSpec as P

F32 = jnp.float32
BF16 = jnp.bfloat16
HEAD_DIM = 64
NORM_EPS = 1e-05
MASKED = -1e30
LOG2E = 1.4426950408889634
GELU_A = 0.7978845608028654
GELU_B = 0.044715


def dot_nn(a, b):
    return jnp.dot(a, b, preferred_element_type=F32)


def dot_nt(a, b):
    return lax.dot_general(a, b, (((1,), (1,)), ((), ())), preferred_element_type=F32)


def dot_tn(a, b):
    return lax.dot_general(a, b, (((0,), (0,)), ((), ())), preferred_element_type=F32)


def dot_tt(a, b):
    return lax.dot_general(a, b, (((0,), (1,)), ((), ())), preferred_element_type=F32)


def norm_parts(inputs):
    row_mean = jnp.mean(inputs, axis=-1, keepdims=True)
    centred = inputs - row_mean
    variance = jnp.mean(centred * centred, axis=-1, keepdims=True)
    inverse = lax.rsqrt(variance + NORM_EPS)
    return centred * inverse, inverse


def norm_back(scaled, normal, inverse):
    return inverse * (
        scaled
        - jnp.mean(scaled, axis=-1, keepdims=True)
        - normal * jnp.mean(scaled * normal, axis=-1, keepdims=True)
    )


def split_three(value):
    high = value.astype(BF16)
    rest = value - high.astype(F32)
    middle = rest.astype(BF16)
    low = (rest - middle.astype(F32)).astype(BF16)
    return high.astype(F32), middle.astype(F32), low.astype(F32)


def scaled_queries(queries):
    scaled = queries.astype(F32) * (LOG2E * HEAD_DIM ** (-0.5))
    high = scaled.astype(BF16)
    return high, (scaled - high.astype(F32)).astype(BF16)


def mask_rows(segments, live, length):
    position = lax.broadcasted_iota(jnp.int32, (16, length), 1)
    row = lax.broadcasted_iota(jnp.int32, (16, length), 0)
    segment = jnp.broadcast_to(segments, (16, length))
    alive = position < live
    for_query = jnp.where(
        row < 8,
        jnp.where(segment != row, MASKED, 0.0),
        jnp.where((row == 8) & alive, MASKED, 0.0),
    )
    for_key = jnp.where(
        row < 8,
        jnp.where(segment == row, 1.0, 0.0),
        jnp.where((row == 8) & (~alive), 1.0, 0.0),
    )
    for_key_back = jnp.where((row >= 9) & (row < 12), 1.0, for_key)
    return for_query, for_key, for_key_back


def head_rows(head, part, width):
    return pl.ds(pl.multiple_of(part * width + head * HEAD_DIM, HEAD_DIM), HEAD_DIM)


def key_band(start, size, tile, length):
    low = max(0, (start - 511) // tile * tile)
    high = min(length, -(-(start + size + 511) // tile) * tile)
    return low, high


def attend_forward(head, qkv_t, ctx_t, lse, mask_q, alive_row, q_aug, k_aug, v_aug, tile):
    width, length = ctx_t.shape
    high, low = scaled_queries(qkv_t[head_rows(head, 0, width), :])
    q_aug[0:64, :] = high
    q_aug[64:128, :] = low
    q_aug[128:144, :] = mask_q[...]
    keys = qkv_t[head_rows(head, 1, width), :]
    k_aug[0:64, :] = keys
    k_aug[64:128, :] = keys
    v_aug[0:64, :] = qkv_t[head_rows(head, 2, width), :]
    for start in range(0, length, tile):
        at = pl.ds(start, tile)
        scores = dot_tn(k_aug[...], q_aug[:, at])
        top = jnp.max(scores, axis=0, keepdims=True)
        weights = jnp.exp2(scores - top).astype(BF16)
        summed = dot_nn(v_aug[...], weights)
        total = summed[64:65, :]
        context = summed[0:64, :] * (1.0 / total)
        own = v_aug[0:64, at].astype(F32)
        ctx_t[head_rows(head, 0, width), at] = jnp.where(
            alive_row[:, at] > 0, context, own
        ).astype(BF16)
        lse[head, :, at] = top + jnp.log(total) * LOG2E


def attend_backward(head, qkv_t, dctx_t, ctx_t, lse, mask_q, q_aug, k_aug, v_aug, d_aug, dk, dv, tile):
    width, length = ctx_t.shape
    scale = HEAD_DIM ** (-0.5)
    row = lax.broadcasted_iota(jnp.int32, (16, length), 0)
    high, low = scaled_queries(qkv_t[head_rows(head, 0, width), :])
    q_aug[0:64, :] = high
    q_aug[64:128, :] = low
    one, two, three = split_three(-lse[head])
    q_aug[128:144, :] = jnp.where(
        row == 9, one, jnp.where(row == 10, two, jnp.where(row == 11, three, mask_q[...].astype(F32)))
    ).astype(BF16)
    keys = qkv_t[head_rows(head, 1, width), :]
    k_aug[0:64, :] = keys
    k_aug[64:128, :] = keys
    v_aug[0:64, :] = qkv_t[head_rows(head, 2, width), :]
    grad = dctx_t[head_rows(head, 0, width), :]
    d_aug[0:64, :] = grad
    context = ctx_t[head_rows(head, 0, width), :].astype(F32)
    one, two, three = split_three(
        -jnp.sum(grad.astype(F32) * context, axis=0, keepdims=True)
    )
    d_aug[64:80, :] = jnp.where(
        row == 0, one, jnp.where(row == 1, two, jnp.where(row == 2, three, 0.0))
    ).astype(BF16)
    dk[...] = jnp.zeros(dk.shape, F32)
    dv[...] = jnp.zeros(dv.shape, F32)
    for start in range(0, length, tile):
        first, last = key_band(start, tile, tile, length)
        at, near = pl.ds(start, tile), pl.ds(first, last - first)
        weights = jnp.exp2(dot_tn(q_aug[:, at], k_aug[:, near]))
        dweights = dot_tn(d_aug[:, at], v_aug[:, near])
        dscores = (weights * dweights).astype(BF16)
        dv[:, near] += dot_nn(d_aug[0:64, at], weights.astype(BF16))
        dk[:, near] += dot_nn(qkv_t[head_rows(head, 0, width), at], dscores)
        qkv_t[head_rows(head, 0, width), at] = (
            dot_nt(k_aug[0:64, near], dscores) * scale
        ).astype(BF16)
    qkv_t[head_rows(head, 1, width), :] = (dk[...] * scale).astype(BF16)
    qkv_t[head_rows(head, 2, width), :] = dv[...].astype(BF16)


def gelu_parts(u):
    square = u * u
    bend = jnp.tanh(u * (GELU_A + (GELU_A * GELU_B) * square))
    half = 0.5 + 0.5 * bend
    slope = half + (0.5 * u) * (1.0 - bend * bend) * (GELU_A + (3.0 * GELU_A * GELU_B) * square)
    return u * half, slope


def kernel(
    tokens, cotangent, segments, live, ln1, ln2, wqkv_in, wattn_in, logits, weights_in,
    out, grad_in, grads_out, qkv_grad, attn_grad, vectors,
    x, dy, wqkv, wattn, w, a1, qkv_t, ctx_t, lse, mid, a2, dz, hid, dpre, z, total, da2,
    dctx_t, qkv_low, attn_low, alive_row, mask_q,
    q_aug, k_aug, v_aug, d_aug, dk, dv, load_sem, store_sem,
):
    length, width = x.shape
    tile = 256
    loads = [
        pltpu.make_async_copy(src, dst, load_sem.at[i])
        for i, (src, dst) in enumerate(
            [(tokens, x), (wqkv_in, wqkv), (wattn_in, wattn), (cotangent, dy), (weights_in, w)]
        )
    ]
    for load in loads:
        load.start()
    live_count = live[0]
    alive_row[...] = jnp.where(
        lax.broadcasted_iota(jnp.int32, (1, length), 1) < live_count, 1.0, 0.0
    )
    for_query, for_key, for_key_back = mask_rows(segments[...], live_count, length)
    mask_q[...] = for_query.astype(BF16)
    k_aug[128:144, :] = for_key.astype(BF16)
    v_aug[64:80, :] = jnp.where(
        lax.broadcasted_iota(jnp.int32, (16, length), 0) == 0, 1.0, 0.0
    ).astype(BF16)
    gain1, bias1 = ln1[0:1, :], ln1[1:2, :]
    gain2, bias2 = ln2[0:1, :], ln2[1:2, :]
    exponent = jnp.exp(logits[...] - jnp.max(logits[...], axis=1, keepdims=True))
    gates = exponent / jnp.sum(exponent, axis=1, keepdims=True)

    loads[0].wait()
    for start in range(0, length, tile):
        at = pl.ds(start, tile)
        normal, inverse = norm_parts(x[at, :].astype(F32))
        a1[at, :] = (normal * gain1 + bias1).astype(BF16)
    loads[1].wait()
    for start in range(0, 3 * width, 512):
        at = pl.ds(start, 512)
        qkv_t[at, :] = dot_tt(wqkv[:, at], a1[...]).astype(BF16)

    def forward_heads(head, carry):
        attend_forward(head, qkv_t, ctx_t, lse, mask_q, alive_row, q_aug, k_aug, v_aug, length)
        return carry

    lax.fori_loop(0, width // HEAD_DIM, forward_heads, 0, unroll=2)

    loads[2].wait()
    loads[3].wait()
    for start in range(0, length, tile):
        at = pl.ds(start, tile)
        middle = x[at, :].astype(F32) + dot_tn(ctx_t[:, at], wattn[...])
        mid[at, :] = middle
        normal, inverse = norm_parts(middle)
        a2[at, :] = (normal * gain2 + bias2).astype(BF16)
        alive = start + lax.broadcasted_iota(jnp.int32, (tile, 1), 0) < live_count
        dy[at, :] = jnp.where(alive, dy[at, :], jnp.zeros((), BF16))
    da2[...] = jnp.zeros(da2.shape, F32)

    loads[4].wait()
    gate_grads = []
    for expert in range(2):
        gate = gates[:, expert : expert + 1]
        for start in range(0, length, tile):
            at = pl.ds(start, tile)
            dz[at, :] = (gate * dy[at, :].astype(F32)).astype(BF16)
        z[...] = jnp.zeros(z.shape, F32)

        def one_half(half, carry):
            slot = 2 * expert + half
            for chunk in range(2):
                w_in, w_out = w.at[slot, 2 * chunk], w.at[slot, 2 * chunk + 1]
                for start in range(0, length, 512):
                    at = pl.ds(start, 512)
                    hidden, slope = gelu_parts(dot_nn(a2[at, :], w_in[...]))
                    hid[chunk, at, :] = hidden.astype(BF16)
                    dpre[chunk, at, :] = (dot_nt(dz[at, :], w_out[...]) * slope).astype(BF16)
                    z[at, :] += dot_nn(hid[chunk, at, :], w_out[...])
                    da2[at, :] += dot_nt(dpre[chunk, at, :], w_in[...])
            for chunk in range(2):
                w[slot, 2 * chunk] = dot_tn(a2[...], dpre[chunk]).astype(BF16)
                w[slot, 2 * chunk + 1] = dot_tn(hid[chunk], dz[...]).astype(BF16)
            return carry

        lax.fori_loop(0, 2, one_half, 0)
        gate_grad = jnp.zeros((1, width), F32)
        for start in range(0, length, tile):
            at = pl.ds(start, tile)
            gate_grad += jnp.sum(dy[at, :].astype(F32) * z[at, :], axis=0, keepdims=True)
            if expert == 0:
                total[at, :] = mid[at, :] + gate * z[at, :]
            else:
                dz[at, :] = (total[at, :] + gate * z[at, :]).astype(BF16)
        gate_grads.append(jnp.sum(gate_grad, axis=1, keepdims=True))
    stores = [
        pltpu.make_async_copy(src, dst, store_sem.at[i])
        for i, (src, dst) in enumerate(
            [(dz, out), (w, grads_out), (attn_low, attn_grad), (qkv_low, qkv_grad), (a2, grad_in)]
        )
    ]
    stores[0].start()
    stores[1].start()

    gain_sum = jnp.zeros((1, width), F32)
    bias_sum = jnp.zeros((1, width), F32)
    for start in range(0, length, tile):
        at = pl.ds(start, tile)
        normal, inverse = norm_parts(mid[at, :])
        grad = da2[at, :]
        gain_sum += jnp.sum(grad * normal, axis=0, keepdims=True)
        bias_sum += jnp.sum(grad, axis=0, keepdims=True)
        dmid = dy[at, :].astype(F32) + norm_back(grad * gain2, normal, inverse)
        mid[at, :] = dmid
        a2[at, :] = dmid.astype(BF16)
    vectors[2:3, :] = gain_sum
    vectors[3:4, :] = bias_sum
    lane = lax.broadcasted_iota(jnp.int32, (1, width), 1)
    vectors[4:5, :] = jnp.where(
        lane == 0, gate_grads[0], jnp.where(lane == 1, gate_grads[1], 0.0)
    )
    vectors[5:8, :] = jnp.zeros((3, width), F32)
    attn_low[...] = dot_nn(ctx_t[...], a2[...]).astype(BF16)
    stores[2].start()
    dctx_t[...] = dot_nt(wattn[...], a2[...]).astype(BF16)

    k_aug[128:144, :] = for_key_back.astype(BF16)
    v_aug[64:80, :] = jnp.where(
        lax.broadcasted_iota(jnp.int32, (16, length), 0) < 3, 1.0, 0.0
    ).astype(BF16)

    def backward_heads(head, carry):
        attend_backward(
            head, qkv_t, dctx_t, ctx_t, lse, mask_q, q_aug, k_aug, v_aug, d_aug, dk, dv, tile
        )
        return carry

    lax.fori_loop(0, width // HEAD_DIM, backward_heads, 0, unroll=2)
    for start in range(0, 3 * width, 512):
        at = pl.ds(start, 512)
        qkv_low[:, at] = dot_tt(a1[...], qkv_t[at, :]).astype(BF16)
    stores[3].start()
    gain_sum = jnp.zeros((1, width), F32)
    bias_sum = jnp.zeros((1, width), F32)
    for start in range(0, length, tile):
        at = pl.ds(start, tile)
        grad = dot_tt(qkv_t[:, at], wqkv[...])
        normal, inverse = norm_parts(x[at, :].astype(F32))
        gain_sum += jnp.sum(grad * normal, axis=0, keepdims=True)
        bias_sum += jnp.sum(grad, axis=0, keepdims=True)
        a2[at, :] = (mid[at, :] + norm_back(grad * gain1, normal, inverse)).astype(BF16)
    vectors[0:1, :] = gain_sum
    vectors[1:2, :] = bias_sum
    stores[4].start()
    for store in stores:
        store.wait()


def one_device(tokens, cotangent, segments, live, ln1, ln2, wqkv, wattn, logits, weights):
    length, width = tokens.shape
    vmem = pl.BlockSpec(memory_space=pltpu.VMEM)
    smem = pl.BlockSpec(memory_space=pltpu.SMEM)
    hbm = pl.BlockSpec(memory_space=pl.ANY)
    shape = jax.ShapeDtypeStruct
    scratch = [
        pltpu.VMEM((length, width), BF16),
        pltpu.VMEM((length, width), BF16),
        pltpu.VMEM(wqkv.shape, BF16),
        pltpu.VMEM(wattn.shape, BF16),
        pltpu.VMEM(weights.shape, BF16),
        pltpu.VMEM((length, width), BF16),
        pltpu.VMEM((3 * width, length), BF16),
        pltpu.VMEM((width, length), BF16),
        pltpu.VMEM((width // HEAD_DIM, 1, length), F32),
        pltpu.VMEM((length, width), F32),
        pltpu.VMEM((length, width), BF16),
        pltpu.VMEM((length, width), BF16),
        pltpu.VMEM((2, length, 512), BF16),
        pltpu.VMEM((2, length, 512), BF16),
        pltpu.VMEM((length, width), F32),
        pltpu.VMEM((length, width), F32),
        pltpu.VMEM((length, width), F32),
        pltpu.VMEM((width, length), BF16),
        pltpu.VMEM(wqkv.shape, BF16),
        pltpu.VMEM(wattn.shape, BF16),
        pltpu.VMEM((1, length), F32),
        pltpu.VMEM((16, length), BF16),
        pltpu.VMEM((144, length), BF16),
        pltpu.VMEM((144, length), BF16),
        pltpu.VMEM((80, length), BF16),
        pltpu.VMEM((80, length), BF16),
        pltpu.VMEM((HEAD_DIM, length), F32),
        pltpu.VMEM((HEAD_DIM, length), F32),
        pltpu.SemaphoreType.DMA((5,)),
        pltpu.SemaphoreType.DMA((5,)),
    ]
    return pl.pallas_call(
        kernel,
        in_specs=[hbm, hbm, vmem, smem, vmem, vmem, hbm, hbm, vmem, hbm],
        out_specs=[hbm, hbm, hbm, hbm, hbm, vmem],
        out_shape=[
            shape(tokens.shape, BF16),
            shape(tokens.shape, BF16),
            shape(weights.shape, BF16),
            shape(wqkv.shape, BF16),
            shape(wattn.shape, BF16),
            shape((8, width), F32),
        ],
        scratch_shapes=scratch,
        compiler_params=pltpu.CompilerParams(vmem_limit_bytes=60 * 1024 * 1024),
    )(tokens, cotangent, segments, live, ln1, ln2, wqkv, wattn, logits, weights)


def to_units(w_in, w_out):
    return jnp.stack([w_in[:, :512], w_out[:512], w_in[:, 512:], w_out[512:]])


def body(
    tokens, segment_ids, live_tokens, cotangent, ln1_gain, ln1_bias, qkv_weight, attn_weight,
    ln2_gain, ln2_bias, task_logits, expert_in, expert_out,
):
    experts = lax.axis_size("expert")
    flip = [(i, i ^ 1) for i in range(experts)]
    up = [(i, (i + 2) % experts) for i in range(experts)]
    down = [((i + 2) % experts, i) for i in range(experts)]
    own = to_units(expert_in[0], expert_out[0])
    following = lax.ppermute(own, "expert", down)
    partner = lax.ppermute(own, "expert", flip)
    following_partner = lax.ppermute(following, "expert", flip)
    weights = jnp.stack([own, partner, following, following_partner])
    ln1 = jnp.stack([ln1_gain, ln1_bias]).astype(F32)
    ln2 = jnp.stack([ln2_gain, ln2_bias]).astype(F32)
    out, grad_in, grads, qkv_grad, attn_grad, vectors = one_device(
        tokens[0], cotangent[0], segment_ids, live_tokens, ln1, ln2, qkv_weight, attn_weight,
        task_logits, weights,
    )
    here = grads[0].astype(F32) + lax.ppermute(grads[1], "expert", flip).astype(F32)
    there = grads[2].astype(F32) + lax.ppermute(grads[3], "expert", flip).astype(F32)
    here = here + lax.ppermute(there.astype(BF16), "expert", up).astype(F32)
    gate_grad = vectors[4, :2]
    here, gate_grad = lax.psum((here, gate_grad), "dp")
    gates = jax.nn.softmax(task_logits[0])
    logits_grad = (gates * (gate_grad - jnp.sum(gates * gate_grad)))[None]
    sums = lax.psum(
        (vectors[:4], qkv_grad.astype(F32), attn_grad.astype(F32)), ("expert", "dp")
    )
    expert_in_grad = jnp.concatenate([here[0], here[2]], axis=1)[None]
    expert_out_grad = jnp.concatenate([here[1], here[3]], axis=0)[None]
    return (
        out[None], grad_in[None], sums[0][0], sums[0][1], sums[1], sums[2], sums[0][2], sums[0][3],
        logits_grad, expert_in_grad, expert_out_grad,
    )


def solution(mesh):
    rows = ("expert", "dp")
    in_specs = (
        P(rows, None, None), P(rows, None), P(rows), P(rows, None, None), P(), P(), P(), P(), P(), P(),
        P("expert", None), P("expert", None, None), P("expert", None, None),
    )
    out_specs = (
        P(rows, None, None), P(rows, None, None), P(), P(), P(), P(), P(), P(),
        P("expert", None), P("expert", None, None), P("expert", None, None),
    )
    return jax.shard_map(body, mesh=mesh, in_specs=in_specs, out_specs=out_specs, check_vma=False)
```

profile of v0, /device:TPU:1, one launch (start us, length us, event | category | flops | bytes accessed | tf_op | source)
XLA Modules:
  0.0 436.0 jit_solution(10538340198283211337)
XLA Ops:
  7.2 0.0 all-reduce.4.cloned.1.call-start
  7.2 1.3 slice_bitcast_fusion.7
  8.6 0.1 copy-done.2
  8.7 0.1 fusion.6
  8.8 0.3 fusion.5
  9.2 4.2 collective-permute-start.1
  13.4 1.2 collective-permute-start
  14.6 43.1 %collective-permute-done.1 = bf16[4,512,512]{2,1,0:T(8,128)(2,1)S(1)} collective-permute-done((bf16[4,512,512]{2,1,0:T(8,128)(2,1)S(1)}, bf16[4,512,512]{2,1,0:T(8,128)(2,1)S(1)}, u32[]{:S(2)}, u32[]{:S(2)}) %collective-permute-start.1) | collective-permute-done | bytes 2097184 | tf_op jit(solution)/shard_map/ppermute | solution.py:395
  57.7 1.2 collective-permute-start.2
  59.6 0.6 maximum_convert_fusion
  60.2 44.3 %collective-permute-done.2 = bf16[4,512,512]{2,1,0:T(8,128)(2,1)S(1)} collective-permute-done((bf16[4,512,512]{2,1,0:T(8,128)(2,1)S(1)}, bf16[4,512,512]{2,1,0:T(8,128)(2,1)S(1)}, u32[]{:S(2)}, u32[]{:S(2)}) %collective-permute-start.2) | collective-permute-done | bytes 2097184 | tf_op jit(solution)/shard_map/ppermute | solution.py:397
  104.6 3.8 pad_maximum_fusion.weights_in
  108.4 79.8 %shard_map.212 = (bf16[1024,512]{1,0:T(8,128)(2,1)}, bf16[1024,512]{1,0:T(8,128)(2,1)}, bf16[4,4,512,512]{3,2,1,0:T(8,128)(2,1)}, bf16[512,1536]{1,0:T(8,128)(2,...) custom-call(bf16[1024,512]{1,0:T(8,128)(2,1)} %bitcast.55, bf16[1024,512]{1,0:T(8,128)(2,1)} %bitcast.56, ...), custom_call_target="tpu_custom_call" | custom-call | tf_op jit(solution)/shard_map/pallas_call | solution.py:365
  188.2 2.7 slice_bitcast_fusion.1
  190.9 1.3 collective-permute-start.4
  192.2 0.3 collective-permute-start.3
  192.4 43.8 %collective-permute-done.4 = bf16[4,512,512]{2,1,0:T(8,128)(2,1)S(1)} collective-permute-done((bf16[4,512,512]{2,1,0:T(8,128)(2,1)S(1)}, bf16[4,512,512]{2,1,0:T(8,128)(2,1)S(1)}, u32[]{:S(2)}, u32[]{:S(2)}) %collective-permute-start.4) | collective-permute-done | bytes 2097184 | tf_op jit(solution)/shard_map/ppermute | solution.py:406
  236.3 0.6 fusion
  236.9 0.1 collective-permute-start.5
  237.0 44.2 %collective-permute-done.3 = bf16[4,512,512]{2,1,0:T(8,128)(2,1)S(1)} collective-permute-done((bf16[4,512,512]{2,1,0:T(8,128)(2,1)S(1)}, bf16[4,512,512]{2,1,0:T(8,128)(2,1)S(1)}, u32[]{:S(2)}, u32[]{:S(2)}) %collective-permute-start.3) | collective-permute-done | bytes 2097184 | tf_op jit(solution)/shard_map/ppermute | solution.py:405
  281.2 2.9 fusion.1
  284.1 0.6 copy-done.5
  284.7 0.6 reduce_max.9
  285.3 1.3 fusion.4
  286.6 10.6 %psum.38 = f32[2]{0:T(128)S(1)} all-reduce(f32[2]{0:T(128)S(1)} %slice_bitcast_fusion.8), channel_id=1, replica_groups=mesh['expert'=8,'dp'=4] {'dp'}, use_global_device_ids=true, to_apply=%region_5.0 | all-reduce | flops 2 | bytes 16 | tf_op jit(solution)/shard_map/psum | solution.py:409
  297.2 122.5 %all-reduce.5 = (f32[4,512]{1,0:T(4,128)S(1)}, f32[512,1536]{1,0:T(8,128)}, f32[512,512]{1,0:T(8,128)}) all-reduce(f32[4,512]{1,0:T(4,128)S(1)} %slice.60, bf16[512,1536]{1,0:T(8,128)(2,1)S(1)} %copy-done.1, bf16[512,512]{1,0:T(8,128)(2,1)S(1)} %copy-done.3), channel_id=1, replica_groups=mesh['expert'=8,'dp'=4] {'expert','dp'}, use_global_device_ids=true, to_apply=%region_0.0 | all-reduce | flops 1050624 | bytes 6307840 | tf_op jit(solution)/shard_map/psum | solution.py:412
  419.7 1.9 fusion.2
  421.6 1.2 fusion.3
  422.7 0.6 fusion.7
  423.3 2.6 slice_bitcast_fusion.3
  425.9 1.5 maximum_bitcast_fusion.1
  427.4 1.5 maximum_bitcast_fusion
  (28 shorter events, 0.1 us)
Async XLA Ops:
  7.2 1.5 copy-start.2
  7.2 416.1 %all-reduce.4.cloned.1.call-start = ((), (), s32[]{:S(2)}) async-start(), calls=%async_computation | async-start | bytes 8388608 | tf_op jit(solution)/shard_map/psum | solution.py:409
  8.8 50.1 %copy-start.6 = (bf16[512]{0:T(512)(128)(2,1)S(1)}, bf16[512]{0:T(512)(128)(2,1)}, u32[]{:S(2)}) copy-start(bf16[512]{0:T(512)(128)(2,1)} %param.17) | copy-start | bytes 3076
  8.8 50.1 %copy-start.7 = (bf16[512]{0:T(512)(128)(2,1)S(1)}, bf16[512]{0:T(512)(128)(2,1)}, u32[]{:S(2)}) copy-start(bf16[512]{0:T(512)(128)(2,1)} %param.18) | copy-start | bytes 3076
  8.8 50.1 %copy-start.8 = (bf16[512]{0:T(512)(128)(2,1)S(1)}, bf16[512]{0:T(512)(128)(2,1)}, u32[]{:S(2)}) copy-start(bf16[512]{0:T(512)(128)(2,1)} %param.21) | copy-start | bytes 3076
  8.8 50.1 %copy-start.9 = (bf16[512]{0:T(512)(128)(2,1)S(1)}, bf16[512]{0:T(512)(128)(2,1)}, u32[]{:S(2)}) copy-start(bf16[512]{0:T(512)(128)(2,1)} %param.22) | copy-start | bytes 3076
  9.2 48.5 %collective-permute-start.1 = (bf16[4,512,512]{2,1,0:T(8,128)(2,1)S(1)}, bf16[4,512,512]{2,1,0:T(8,128)(2,1)S(1)}, u32[]{:S(2)}, u32[]{:S(2)}) collective-permute-start(bf16[4,512,512]{2,1,0:T(8,128)(2,1)S(1)} %get-tuple-element.35), channel_id=1, source_target_pairs={{8,0},{12,4},{16,8},{20,12},{24,16},{28,20},{0,24},{4,28},{9,1},{1... | collective-permute-start | bytes 6291464 | tf_op jit(solution)/shard_map/ppermute | solution.py:395
  13.4 46.8 %collective-permute-start = (bf16[4,512,512]{2,1,0:T(8,128)(2,1)S(1)}, bf16[4,512,512]{2,1,0:T(8,128)(2,1)S(1)}, u32[]{:S(2)}, u32[]{:S(2)}) collective-permute-start(bf16[4,512,512]{2,1,0:T(8,128)(2,1)S(1)} %get-tuple-element.35), channel_id=1, source_target_pairs={{0,4},{4,0},{8,12},{12,8},{16,20},{20,16},{24,28},{28,24},{1,5},{5... | collective-permute-start | bytes 6291464 | tf_op jit(solution)/shard_map/ppermute | solution.py:396
  57.7 46.9 %collective-permute-start.2 = (bf16[4,512,512]{2,1,0:T(8,128)(2,1)S(1)}, bf16[4,512,512]{2,1,0:T(8,128)(2,1)S(1)}, u32[]{:S(2)}, u32[]{:S(2)}) collective-permute-start(bf16[4,512,512]{2,1,0:T(8,128)(2,1)S(1)} %collective-permute-done.1), channel_id=1, source_target_pairs={{0,4},{4,0},{8,12},{12,8},{16,20},{20,16},{24,28},{28,24},{1,5},{5... | collective-permute-start | bytes 6291464 | tf_op jit(solution)/shard_map/ppermute | solution.py:397
  188.2 48.0 %copy-start = (bf16[4,4,512,512]{3,2,1,0:T(8,128)(2,1)S(1)}, bf16[4,4,512,512]{3,2,1,0:T(8,128)(2,1)}, u32[]{:S(2)}) copy-start(bf16[4,4,512,512]{3,2,1,0:T(8,128)(2,1)} %get-tuple-element.22) | copy-start | bytes 25165828
  190.9 45.4 %collective-permute-start.4 = (bf16[4,512,512]{2,1,0:T(8,128)(2,1)S(1)}, bf16[4,512,512]{2,1,0:T(8,128)(2,1)S(1)}, u32[]{:S(2)}, u32[]{:S(2)}) collective-permute-start(bf16[4,512,512]{2,1,0:T(8,128)(2,1)S(1)} %get-tuple-element.29), channel_id=1, source_target_pairs={{0,4},{4,0},{8,12},{12,8},{16,20},{20,16},{24,28},{28,24},{1,5},{5... | collective-permute-start | bytes 6291464 | tf_op jit(solution)/shard_map/ppermute | solution.py:406
  192.2 89.0 %collective-permute-start.3 = (bf16[4,512,512]{2,1,0:T(8,128)(2,1)S(1)}, bf16[4,512,512]{2,1,0:T(8,128)(2,1)S(1)}, u32[]{:S(2)}, u32[]{:S(2)}) collective-permute-start(bf16[4,512,512]{2,1,0:T(8,128)(2,1)S(1)} %get-tuple-element.28), channel_id=1, source_target_pairs={{0,4},{4,0},{8,12},{12,8},{16,20},{20,16},{24,28},{28,24},{1,5},{5... | collective-permute-start | bytes 6291464 | tf_op jit(solution)/shard_map/ppermute | solution.py:405
  236.9 44.3 %collective-permute-start.5 = (bf16[4,512,512]{2,1,0:T(8,128)(2,1)S(1)}, bf16[4,512,512]{2,1,0:T(8,128)(2,1)S(1)}, u32[]{:S(2)}, u32[]{:S(2)}) collective-permute-start(bf16[4,512,512]{2,1,0:T(8,128)(2,1)S(1)} %fusion), channel_id=1, source_target_pairs={{0,8},{4,12},{8,16},{12,20},{16,24},{20,28},{24,0},{28,4},{1,9},{5... | collective-permute-start | bytes 6291464 | tf_op jit(solution)/shard_map/ppermute | solution.py:407
  284.1 0.7 copy-start.5
  284.1 1.3 copy-start.4
  284.1 13.1 %copy-start.1 = (bf16[512,1536]{1,0:T(8,128)(2,1)S(1)}, bf16[512,1536]{1,0:T(8,128)(2,1)}, u32[]{:S(2)}) copy-start(bf16[512,1536]{1,0:T(8,128)(2,1)} %get-tuple-element.20) | copy-start | bytes 4718596
  284.1 13.1 %copy-start.3 = (bf16[512,512]{1,0:T(8,128)(2,1)S(1)}, bf16[512,512]{1,0:T(8,128)(2,1)}, u32[]{:S(2)}) copy-start(bf16[512,512]{1,0:T(8,128)(2,1)} %get-tuple-element.21) | copy-start | bytes 1572868
Sparse Core Ops, SparseCore 0:
  284.2 116.1 all-reduce.3
where the time goes:
time: 444 us; the launch traced here: 436 us
  waiting for transfers between devices  176 us (40%)
  blocking collectives  133 us (30%)
  Pallas kernels  79.8 us (18%)
  other arithmetic  16.2 us (4%)
  between operations  15.1 us (3%)
  starting transfers between devices  8.25 us (2%)
  local copies, waits for them, and re-layouts  8.1 us (2%)
    psum x1, blocking collectives, body(): lax.psum((vectors[:4], qkv_grad.astype(F32), attn_grad.astype(F32)), ('ex...  123 us
    pallas_call x1, Pallas kernels, one_device(): pl.pallas_call(kernel, in_specs=[hbm, hbm, vmem, smem, vmem, vmem, hbm, h...  79.8 us
    ppermute x1, waiting for transfers between devices, body(): following_partner = lax.ppermute(following, 'expert', flip)  44.3 us
    ppermute x1, waiting for transfers between devices, body(): lax.ppermute(grads[1], 'expert', flip).astype(F32)  44.2 us
    ppermute x1, waiting for transfers between devices, body(): lax.ppermute(grads[3], 'expert', flip).astype(F32)  43.8 us
    ppermute x1, waiting for transfers between devices, body(): following = lax.ppermute(own, 'expert', down)  43.1 us
    psum x1, blocking collectives, body(): here, gate_grad = lax.psum((here, gate_grad), 'dp')  10.6 us
  transfers between devices with their start and end apart: 7, of which 4 were waited for; matrix products, arithmetic and copies ran while one was open for 2% of the time, Pallas kernels for 0%

commit v1 on v0

--- a/solution.py
+++ b/solution.py
@@ -166,19 +166,75 @@
     return u * half, slope
 
 
+MESH = pl.DeviceIdType.MESH
+GROUP = 8
+
+W1X, W1Y, W1C, W1D, W2A, W2B, W2C, W2D = 0, 2, 4, 5, 6, 7, 8, 9
+W3X, W3Y, W3C, W3D = 10, 11, 12, 13
+GC, GX, GZ, GY, GF = 14, 22, 30, 34, 38
+SUM, SUM_STEP = 42, 18
+VD, VE = 78, 81
+CROSS = 88
+
+
 def kernel(
-    tokens, cotangent, segments, live, ln1, ln2, wqkv_in, wattn_in, logits, weights_in,
-    out, grad_in, grads_out, qkv_grad, attn_grad, vectors,
+    experts,
+    tokens, cotangent, segments, live, ln1, ln2, wqkv_in, wattn_in, logits, expert_in, expert_out,
+    out, grad_in, in_grad, out_grad, qkv_grad, attn_grad, vectors, logits_grad,
     x, dy, wqkv, wattn, w, a1, qkv_t, ctx_t, lse, mid, a2, dz, hid, dpre, z, total, da2,
-    dctx_t, qkv_low, attn_low, alive_row, mask_q,
-    q_aug, k_aug, v_aug, d_aug, dk, dv, load_sem, store_sem,
+    dctx_t, alive_row, mask_q, q_aug, k_aug, v_aug, d_aug, dk, dv,
+    rc, rx, rz, ry, fin, part, ac, ay, ae, across, done, vec_dp, vec_ex,
+    load_sem, store_sem, send_sem, recv_sem,
 ):
     length, width = x.shape
     tile = 256
+    expert = lax.axis_index("expert")
+    dp = lax.axis_index("dp")
+    core, row_y = dp % 2, dp // 2
+    dp_core = dp + 1 - 2 * core
+    dp_y = (dp + 2) % 4
+    place = expert % GROUP
+    base = expert - place
+    mate_core = (expert, dp_core)
+    mate_y = (expert, dp_y)
+    mate_x = (expert + 1 - 2 * (expert % 2), dp)
+    above = ((expert + 2) % experts, dp)
+    below = ((expert + experts - 2) % experts, dp)
+    groups = experts // GROUP
+
+    def copy(src, dst, index, device):
+        return pltpu.make_async_remote_copy(
+            src_ref=src, dst_ref=dst, send_sem=send_sem.at[index], recv_sem=recv_sem.at[index],
+            device_id=device, device_id_type=MESH,
+        )
+
+    def peer(step):
+        return (base + (place + step) % GROUP, dp)
+
+    def far(step):
+        return ((expert + GROUP * step) % experts, dp)
+
+    barrier = pltpu.get_barrier_semaphore()
+    others = [mate_core, mate_y, (expert, (dp_core + 2) % 4)]
+    others += [peer(step) for step in range(1, GROUP)]
+    if groups > 1:
+        others += [above, below] + [far(step) for step in range(1, groups)]
+    for other in others:
+        pl.semaphore_signal(barrier, inc=1, device_id=other, device_id_type=MESH)
+
     loads = [
         pltpu.make_async_copy(src, dst, load_sem.at[i])
         for i, (src, dst) in enumerate(
-            [(tokens, x), (wqkv_in, wqkv), (wattn_in, wattn), (cotangent, dy), (weights_in, w)]
+            [
+                (expert_in.at[:, pl.ds(0, 512)], w.at[0, 0]),
+                (expert_out.at[pl.ds(0, 512), :], w.at[0, 1]),
+                (expert_in.at[:, pl.ds(512, 512)], w.at[0, 2]),
+                (expert_out.at[pl.ds(512, 512), :], w.at[0, 3]),
+                (tokens, x),
+                (wqkv_in, wqkv),
+                (wattn_in, wattn),
+                (cotangent, dy),
+            ]
         )
     ]
     for load in loads:
@@ -198,24 +254,67 @@
     exponent = jnp.exp(logits[...] - jnp.max(logits[...], axis=1, keepdims=True))
     gates = exponent / jnp.sum(exponent, axis=1, keepdims=True)
 
-    loads[0].wait()
+    def half(ref, index, part_index):
+        return ref.at[index[0], index[1], pl.ds(256 * part_index, 256), :]
+
+    w1x = [copy(half(w, (0, dp), h), half(w, (1, dp), h), W1X + h, mate_x) for h in range(2)]
+    w1y = [copy(half(w, (1, dp), h), half(w, (1, dp), h), W1Y + h, mate_y) for h in range(2)]
+    w1c = copy(w.at[1, dp], w.at[1, dp], W1C, mate_core)
+    w1d = copy(w.at[1, dp_y], w.at[1, dp_y], W1D, mate_core)
+    w2a = copy(w.at[0, dp], w.at[2, dp], W2A, below)
+    w2b = copy(w.at[0, dp_y], w.at[2, dp_y], W2B, below)
+    w2c = copy(w.at[2, dp], w.at[2, dp], W2C, mate_core)
+    w2d = copy(w.at[2, dp_y], w.at[2, dp_y], W2D, mate_core)
+    w3x = copy(w.at[2, dp], w.at[3, dp], W3X, mate_x)
+    w3y = copy(w.at[3, dp], w.at[3, dp], W3Y, mate_y)
+    w3c = copy(w.at[3, dp], w.at[3, dp], W3C, mate_core)
+    w3d = copy(w.at[3, dp_y], w.at[3, dp_y], W3D, mate_core)
+
+    for load in loads[:4]:
+        load.wait()
+    pl.semaphore_wait(barrier, len(others))
+    w1x[0].start()
+    w2a.start()
+    w1x[1].start()
+
+    loads[4].wait()
     for start in range(0, length, tile):
         at = pl.ds(start, tile)
         normal, inverse = norm_parts(x[at, :].astype(F32))
         a1[at, :] = (normal * gain1 + bias1).astype(BF16)
-    loads[1].wait()
+    loads[5].wait()
     for start in range(0, 3 * width, 512):
         at = pl.ds(start, 512)
         qkv_t[at, :] = dot_tt(wqkv[:, at], a1[...]).astype(BF16)
 
-    def forward_heads(head, carry):
-        attend_forward(head, qkv_t, ctx_t, lse, mask_q, alive_row, q_aug, k_aug, v_aug, length)
+    def forward_heads(pair, carry):
+        @pl.when(pair == 1)
+        def _():
+            w2b.start()
+
+        @pl.when(pair == 2)
+        def _():
+            w1x[0].wait_recv()
+            w1y[0].start()
+
+        @pl.when(pair == 3)
+        def _():
+            w2a.wait_recv()
+            w3x.start()
+            w1x[1].wait_recv()
+            w1y[1].start()
+            w1c.start()
+
+        for head in range(2):
+            attend_forward(
+                2 * pair + head, qkv_t, ctx_t, lse, mask_q, alive_row, q_aug, k_aug, v_aug, length
+            )
         return carry
 
-    lax.fori_loop(0, width // HEAD_DIM, forward_heads, 0, unroll=2)
-
-    loads[2].wait()
-    loads[3].wait()
+    lax.fori_loop(0, width // HEAD_DIM // 2, forward_heads, 0)
+
+    loads[6].wait()
+    loads[7].wait()
     for start in range(0, length, tile):
         at = pl.ds(start, tile)
         middle = x[at, :].astype(F32) + dot_tn(ctx_t[:, at], wattn[...])
@@ -226,49 +325,136 @@
         dy[at, :] = jnp.where(alive, dy[at, :], jnp.zeros((), BF16))
     da2[...] = jnp.zeros(da2.shape, F32)
 
-    loads[4].wait()
-    gate_grads = []
-    for expert in range(2):
-        gate = gates[:, expert : expert + 1]
-        for start in range(0, length, tile):
-            at = pl.ds(start, tile)
-            dz[at, :] = (gate * dy[at, :].astype(F32)).astype(BF16)
-        z[...] = jnp.zeros(z.shape, F32)
-
-        def one_half(half, carry):
-            slot = 2 * expert + half
-            for chunk in range(2):
-                w_in, w_out = w.at[slot, 2 * chunk], w.at[slot, 2 * chunk + 1]
-                for start in range(0, length, 512):
-                    at = pl.ds(start, 512)
-                    hidden, slope = gelu_parts(dot_nn(a2[at, :], w_in[...]))
-                    hid[chunk, at, :] = hidden.astype(BF16)
-                    dpre[chunk, at, :] = (dot_nt(dz[at, :], w_out[...]) * slope).astype(BF16)
-                    z[at, :] += dot_nn(hid[chunk, at, :], w_out[...])
-                    da2[at, :] += dot_nt(dpre[chunk, at, :], w_in[...])
-            for chunk in range(2):
-                w[slot, 2 * chunk] = dot_tn(a2[...], dpre[chunk]).astype(BF16)
-                w[slot, 2 * chunk + 1] = dot_tn(hid[chunk], dz[...]).astype(BF16)
-            return carry
-
-        lax.fori_loop(0, 2, one_half, 0)
-        gate_grad = jnp.zeros((1, width), F32)
-        for start in range(0, length, tile):
-            at = pl.ds(start, tile)
-            gate_grad += jnp.sum(dy[at, :].astype(F32) * z[at, :], axis=0, keepdims=True)
-            if expert == 0:
-                total[at, :] = mid[at, :] + gate * z[at, :]
-            else:
-                dz[at, :] = (total[at, :] + gate * z[at, :]).astype(BF16)
-        gate_grads.append(jnp.sum(gate_grad, axis=1, keepdims=True))
-    stores = [
-        pltpu.make_async_copy(src, dst, store_sem.at[i])
-        for i, (src, dst) in enumerate(
-            [(dz, out), (w, grads_out), (attn_low, attn_grad), (qkv_low, qkv_grad), (a2, grad_in)]
+    def add_into(target, *terms):
+        value = target[...].astype(F32)
+        for term in terms:
+            value = value + term[...].astype(F32)
+        target[...] = value.astype(BF16)
+
+    def gc(slot, chunk):
+        return copy(
+            w.at[slot, 2 * chunk + 1 - core], rc.at[slot, chunk], GC + 2 * slot + chunk, mate_core
         )
+
+    def add_core(slot):
+        for chunk in range(2):
+            gc(slot, chunk).wait_recv()
+            add_into(w.at[slot, 2 * chunk + core], rc.at[slot, chunk])
+
+    def piece(ref, slot, index):
+        chunk, part_index = index // 2, index % 2
+        return ref.at[slot, 2 * chunk + core, pl.ds(256 * part_index, 256), :]
+
+    def landed(ref, index):
+        return ref.at[index // 2, pl.ds(256 * (index % 2), 256), :]
+
+    gx = [
+        [copy(piece(w, 2 * s + 1, i), landed(rx.at[s], i), GX + 4 * s + i, mate_x) for i in range(4)]
+        for s in range(2)
     ]
+    gz = [copy(piece(w, 2, i), landed(rz, i), GZ + i, above) for i in range(4)]
+    gy = [copy(piece(w, 0, i), landed(ry, i), GY + i, mate_y) for i in range(4)]
+
+    def final(index):
+        chunk, part_index = index // 2, index % 2
+        return fin.at[2 * chunk + core, pl.ds(256 * part_index, 256), :]
+
+    gf = [copy(final(i), final(i), GF + i, mate_core) for i in range(4)]
+
+    def one_slot(slot, carry):
+        gate = jnp.where(slot < 2, gates[:, 0:1], gates[:, 1:2])
+
+        @pl.when(slot == 1)
+        def _():
+            w1y[0].wait_recv()
+            w1y[1].wait_recv()
+            w1d.start()
+            w3x.wait_recv()
+            w3y.start()
+            w3c.start()
+            w1c.wait_recv()
+            w1d.wait_recv()
+
+        @pl.when(slot == 2)
+        def _():
+            w2b.wait_recv()
+            w2d.start()
+            w2c.start()
+            w2c.wait_recv()
+            w2d.wait_recv()
+
+        @pl.when(slot == 3)
+        def _():
+            w3c.wait_recv()
+            w3d.wait_recv()
+
+        @pl.when(slot % 2 == 0)
+        def _():
+            for start in range(0, length, tile):
+                at = pl.ds(start, tile)
+                dz[at, :] = (gate * dy[at, :].astype(F32)).astype(BF16)
+            z[...] = jnp.zeros(z.shape, F32)
+
+        for chunk in range(2):
+            w_in, w_out = w.at[slot, 2 * chunk], w.at[slot, 2 * chunk + 1]
+            for start in range(0, length, 512):
+                at = pl.ds(start, 512)
+                hidden, slope = gelu_parts(dot_nn(a2[at, :], w_in[...]))
+                hid[chunk, at, :] = hidden.astype(BF16)
+                dpre[chunk, at, :] = (dot_nt(dz[at, :], w_out[...]) * slope).astype(BF16)
+                z[at, :] += dot_nn(hid[chunk, at, :], w_out[...])
+                da2[at, :] += dot_nt(dpre[chunk, at, :], w_in[...])
+
+        @pl.when(slot == 0)
+        def _():
+            for each in w1x + [w2a, w2b]:
+                each.wait_send()
+
+        @pl.when(slot == 1)
+        def _():
+            for each in w1y + [w1c, w1d]:
+                each.wait_send()
+            add_core(0)
+
+        @pl.when(slot == 2)
+        def _():
+            for each in [w3x, w2c, w2d]:
+                each.wait_send()
+            w3y.wait_recv()
+            w3d.start()
+            add_core(1)
+            for each in gx[0]:
+                each.start()
+
+        @pl.when(slot == 3)
+        def _():
+            for each in [w3y, w3c, w3d]:
+                each.wait_send()
+            add_core(2)
+
+        for chunk in range(2):
+            w[slot, 2 * chunk] = dot_tn(a2[...], dpre[chunk]).astype(BF16)
+            w[slot, 2 * chunk + 1] = dot_tn(hid[chunk], dz[...]).astype(BF16)
+            gc(slot, chunk).start()
+
+        @pl.when(slot % 2 == 1)
+        def _():
+            gate_grad = jnp.zeros((1, width), F32)
+            for start in range(0, length, tile):
+                at = pl.ds(start, tile)
+                branch = z[at, :]
+                gate_grad += jnp.sum(dy[at, :].astype(F32) * branch, axis=0, keepdims=True)
+                previous = jnp.where(slot == 1, mid[at, :], total[at, :])
+                total[at, :] = previous + gate * branch
+            vectors[pl.ds(4, 1), :] = jnp.where(slot == 1, gate_grad, vectors[pl.ds(4, 1), :])
+            vectors[pl.ds(5, 1), :] = gate_grad
+
+        return carry
+
+    lax.fori_loop(0, 4, one_slot, 0)
+    dz[...] = total[...].astype(BF16)
+    stores = [pltpu.make_async_copy(dz, out, store_sem.at[0])]
     stores[0].start()
-    stores[1].start()
 
     gain_sum = jnp.zeros((1, width), F32)
     bias_sum = jnp.zeros((1, width), F32)
@@ -283,31 +469,155 @@
         a2[at, :] = dmid.astype(BF16)
     vectors[2:3, :] = gain_sum
     vectors[3:4, :] = bias_sum
-    lane = lax.broadcasted_iota(jnp.int32, (1, width), 1)
-    vectors[4:5, :] = jnp.where(
-        lane == 0, gate_grads[0], jnp.where(lane == 1, gate_grads[1], 0.0)
-    )
-    vectors[5:8, :] = jnp.zeros((3, width), F32)
-    attn_low[...] = dot_nn(ctx_t[...], a2[...]).astype(BF16)
-    stores[2].start()
+    vectors[6:8, :] = jnp.zeros((2, width), F32)
+    add_core(3)
+    for each in gx[1]:
+        each.start()
+    for block in range(2):
+        part[block] = dot_nn(ctx_t[...], a2[:, 256 * block : 256 * block + 256]).astype(BF16)
     dctx_t[...] = dot_nt(wattn[...], a2[...]).astype(BF16)
+
+    def sum_round(index, low, high):
+        blocks = pl.ds(low, high - low)
+        first = SUM + SUM_STEP * index
+        own_half = pl.ds(pl.multiple_of(256 * core, 256), 256)
+        other_half = pl.ds(pl.multiple_of(256 * (1 - core), 256), 256)
+        corner = 256 * core + 128 * row_y
+        own_quarter = pl.ds(pl.multiple_of(corner, 128), 128)
+        other_quarter = pl.ds(pl.multiple_of(256 * core + 128 * (1 - row_y), 128), 128)
+
+        def rows(step):
+            return pl.ds(pl.multiple_of(corner + 16 * ((place + step) % GROUP), 16), 16)
+
+        to_core = copy(part.at[blocks, other_half, :], ac.at[blocks], first, mate_core)
+        to_y = copy(part.at[blocks, other_quarter, :], ay.at[blocks], first + 1, mate_y)
+        spread = [
+            copy(part.at[blocks, rows(s), :], ae.at[s, blocks], first + 1 + s, peer(s))
+            for s in range(1, GROUP)
+        ]
+        gather = [
+            copy(done.at[blocks, rows(0), :], done.at[blocks, rows(0), :], first + 8 + s, peer(s))
+            for s in range(1, GROUP)
+        ]
+        back_y = copy(done.at[blocks, own_quarter, :], done.at[blocks, own_quarter, :], first + 16, mate_y)
+        back_core = copy(done.at[blocks, own_half, :], done.at[blocks, own_half, :], first + 17, mate_core)
+        over = [
+            copy(across.at[0, blocks], across.at[s, blocks], CROSS + (groups - 1) * index + s - 1, far(s))
+            for s in range(1, groups)
+        ]
+
+        def step_core():
+            to_core.start()
+
+        def step_y():
+            to_core.wait_recv()
+            add_into(part.at[blocks, own_half, :], ac.at[blocks])
+            to_y.start()
+
+        def step_spread():
+            to_y.wait_recv()
+            add_into(part.at[blocks, own_quarter, :], ay.at[blocks])
+            for each in spread:
+                each.start()
+
+        def step_gather():
+            for each in spread:
+                each.wait_recv()
+            value = part[blocks, rows(0), :].astype(F32)
+            for s in range(1, GROUP):
+                value = value + ae[s, blocks].astype(F32)
+            if groups > 1:
+                across[0, blocks] = value.astype(BF16)
+                for each in over:
+                    each.start()
+                for each in over:
+                    each.wait_recv()
+                value = jnp.zeros(value.shape, F32)
+
+                def add_group(group, value):
+                    step = (expert // GROUP - group + groups) % groups
+                    return value + across[step, blocks].astype(F32)
+
+                value = lax.fori_loop(0, groups, add_group, value)
+            done[blocks, rows(0), :] = value.astype(BF16)
+            for each in gather:
+                each.start()
+
+        def step_back_y():
+            for each in gather:
+                each.wait_recv()
+            back_y.start()
+
+        def step_back_core():
+            back_y.wait_recv()
+            back_core.start()
+
+        def step_end():
+            back_core.wait_recv()
+
+        def finish():
+            for each in [to_core, to_y, back_y, back_core] + spread + gather + over:
+                each.wait_send()
+
+        return step_core, step_y, step_spread, step_gather, step_back_y, step_back_core, step_end, finish
+
+    round_a = sum_round(0, 0, 5)
+    round_b = sum_round(1, 5, 8)
 
     k_aug[128:144, :] = for_key_back.astype(BF16)
     v_aug[64:80, :] = jnp.where(
         lax.broadcasted_iota(jnp.int32, (16, length), 0) < 3, 1.0, 0.0
     ).astype(BF16)
 
-    def backward_heads(head, carry):
-        attend_backward(
-            head, qkv_t, dctx_t, ctx_t, lse, mask_q, q_aug, k_aug, v_aug, d_aug, dk, dv, tile
-        )
+    def qkv_blocks(first, offset):
+        for index in range(3):
+            at = pl.ds(index * width + offset, 256)
+            part[first + index] = dot_tt(a1[...], qkv_t[at, :]).astype(BF16)
+
+    def pass_on_z(index):
+        gx[1][index].wait_recv()
+        add_into(piece(w, 2, index), landed(rx.at[1], index))
+        gz[index].start()
+
+    def pass_on_y(index):
+        gz[index].wait_recv()
+        add_into(piece(w, 0, index), landed(rz, index))
+        gy[index].start()
+
+    def pass_on_core(index):
+        gy[index].wait_recv()
+        final(index)[...] = (
+            piece(w, 0, index)[...].astype(F32) + landed(ry, index)[...].astype(F32)
+        ).astype(BF16)
+        gf[index].start()
+
+    def backward_heads(pair, carry):
+        @pl.when(pair == 2)
+        def _():
+            qkv_blocks(2, 0)
+            round_a[0]()
+            for index in range(4):
+                gx[0][index].wait_recv()
+                add_into(piece(w, 0, index), landed(rx.at[0], index))
+
+        @pl.when(pair == 3)
+        def _():
+            round_a[1]()
+            pass_on_z(0)
+
+        for head in range(2):
+            attend_backward(
+                2 * pair + head, qkv_t, dctx_t, ctx_t, lse, mask_q, q_aug, k_aug, v_aug, d_aug,
+                dk, dv, tile,
+            )
         return carry
 
-    lax.fori_loop(0, width // HEAD_DIM, backward_heads, 0, unroll=2)
-    for start in range(0, 3 * width, 512):
-        at = pl.ds(start, 512)
-        qkv_low[:, at] = dot_tt(a1[...], qkv_t[at, :]).astype(BF16)
-    stores[3].start()
+    lax.fori_loop(0, width // HEAD_DIM // 2, backward_heads, 0)
+    qkv_blocks(5, 256)
+    round_b[0]()
+    round_a[2]()
+    pass_on_z(1)
+
     gain_sum = jnp.zeros((1, width), F32)
     bias_sum = jnp.zeros((1, width), F32)
     for start in range(0, length, tile):
@@ -317,25 +627,128 @@
         gain_sum += jnp.sum(grad * normal, axis=0, keepdims=True)
         bias_sum += jnp.sum(grad, axis=0, keepdims=True)
         a2[at, :] = (mid[at, :] + norm_back(grad * gain1, normal, inverse)).astype(BF16)
+        if start == tile:
+            round_b[1]()
+            round_a[3]()
+            pass_on_z(2)
+    stores.append(pltpu.make_async_copy(a2, grad_in, store_sem.at[1]))
+    stores[1].start()
+    lane = lax.broadcasted_iota(jnp.int32, (1, width), 1)
     vectors[0:1, :] = gain_sum
     vectors[1:2, :] = bias_sum
-    stores[4].start()
+
+    vec_dp[dp] = vectors[...]
+    to_dp = [
+        copy(vec_dp.at[dp], vec_dp.at[dp], VD + s - 1, (expert, (dp + s) % 4)) for s in range(1, 4)
+    ]
+    for each in to_dp:
+        each.start()
+    round_b[2]()
+    pass_on_z(3)
+    pass_on_y(0)
+    for each in to_dp:
+        each.wait_recv()
+    row_sum = vec_dp[0] + vec_dp[1] + vec_dp[2] + vec_dp[3]
+    vec_ex[expert] = row_sum
+    to_ex = [
+        copy(vec_ex.at[expert], vec_ex.at[expert], VE + s - 1, peer(s)) for s in range(1, GROUP)
+    ]
+    for each in to_ex:
+        each.start()
+    gate_sums = jnp.sum(row_sum[4:6, :], axis=1, keepdims=True)
+    pair_lane = lax.broadcasted_iota(jnp.int32, (1, 2), 1)
+    dgate = jnp.where(pair_lane == 0, gate_sums[0:1, :], gate_sums[1:2, :])
+    logits_grad[...] = gates * (dgate - jnp.sum(gates * dgate, axis=1, keepdims=True))
+
+    round_a[4]()
+    pass_on_y(1)
+    round_b[3]()
+    pass_on_y(2)
+    round_a[5]()
+    pass_on_core(0)
+    pass_on_y(3)
+    round_b[4]()
+    pass_on_core(1)
+    for each in to_ex:
+        each.wait_recv()
+    sums = [to_dp, to_ex]
+    if groups > 1:
+        vec_group = vec_ex[base]
+        for s in range(1, GROUP):
+            vec_group = vec_group + vec_ex[base + s]
+        vec_ex[experts + expert // GROUP] = vec_group
+        to_far = [
+            copy(
+                vec_ex.at[experts + expert // GROUP], vec_ex.at[experts + expert // GROUP],
+                CROSS + 2 * (groups - 1) + s - 1, far(s),
+            )
+            for s in range(1, groups)
+        ]
+        for each in to_far:
+            each.start()
+        for each in to_far:
+            each.wait_recv()
+        sums.append(to_far)
+        value = vec_ex[experts]
+        for s in range(1, groups):
+            value = value + vec_ex[experts + s]
+    else:
+        value = vec_ex[0]
+        for s in range(1, GROUP):
+            value = value + vec_ex[s]
+    vectors[...] = value
+    pass_on_core(2)
+    round_a[6]()
+    for block in range(5):
+        if block < 2:
+            target = attn_grad.at[:, pl.ds(256 * block, 256)]
+        else:
+            target = qkv_grad.at[:, pl.ds((block - 2) * width, 256)]
+        stores.append(pltpu.make_async_copy(done.at[block], target, store_sem.at[2 + block]))
+        stores[-1].start()
+    round_b[5]()
+    pass_on_core(3)
+    round_b[6]()
+    for block in range(3):
+        target = qkv_grad.at[:, pl.ds(block * width + 256, 256)]
+        stores.append(pltpu.make_async_copy(done.at[5 + block], target, store_sem.at[7 + block]))
+        stores[-1].start()
+    for each in gf:
+        each.wait_recv()
+    for chunk in range(2):
+        at = pl.ds(512 * chunk, 512)
+        for kind, target in enumerate([in_grad.at[:, at], out_grad.at[at, :]]):
+            index = 2 * chunk + kind
+            stores.append(pltpu.make_async_copy(fin.at[index], target, store_sem.at[10 + index]))
+            stores[-1].start()
+    for slot in range(4):
+        for chunk in range(2):
+            gc(slot, chunk).wait_send()
+    for group in [gx[0], gx[1], gz, gy, gf] + sums:
+        for each in group:
+            each.wait_send()
+    round_a[7]()
+    round_b[7]()
     for store in stores:
         store.wait()
 
 
-def one_device(tokens, cotangent, segments, live, ln1, ln2, wqkv, wattn, logits, weights):
+def one_device(
+    experts, tokens, cotangent, segments, live, ln1, ln2, wqkv, wattn, logits, expert_in, expert_out
+):
     length, width = tokens.shape
+    groups = experts // GROUP
     vmem = pl.BlockSpec(memory_space=pltpu.VMEM)
     smem = pl.BlockSpec(memory_space=pltpu.SMEM)
     hbm = pl.BlockSpec(memory_space=pl.ANY)
     shape = jax.ShapeDtypeStruct
+    semaphores = CROSS + 3 * (groups - 1)
     scratch = [
         pltpu.VMEM((length, width), BF16),
         pltpu.VMEM((length, width), BF16),
         pltpu.VMEM(wqkv.shape, BF16),
         pltpu.VMEM(wattn.shape, BF16),
-        pltpu.VMEM(weights.shape, BF16),
+        pltpu.VMEM((4, 4, 512, 512), BF16),
         pltpu.VMEM((length, width), BF16),
         pltpu.VMEM((3 * width, length), BF16),
         pltpu.VMEM((width, length), BF16),
@@ -349,8 +762,6 @@
         pltpu.VMEM((length, width), F32),
         pltpu.VMEM((length, width), F32),
         pltpu.VMEM((width, length), BF16),
-        pltpu.VMEM(wqkv.shape, BF16),
-        pltpu.VMEM(wattn.shape, BF16),
         pltpu.VMEM((1, length), F32),
         pltpu.VMEM((16, length), BF16),
         pltpu.VMEM((144, length), BF16),
@@ -359,64 +770,59 @@
         pltpu.VMEM((80, length), BF16),
         pltpu.VMEM((HEAD_DIM, length), F32),
         pltpu.VMEM((HEAD_DIM, length), F32),
-        pltpu.SemaphoreType.DMA((5,)),
-        pltpu.SemaphoreType.DMA((5,)),
+        pltpu.VMEM((4, 2, 512, 512), BF16),
+        pltpu.VMEM((2, 2, 512, 512), BF16),
+        pltpu.VMEM((2, 512, 512), BF16),
+        pltpu.VMEM((2, 512, 512), BF16),
+        pltpu.VMEM((4, 512, 512), BF16),
+        pltpu.VMEM((8, 512, 256), BF16),
+        pltpu.VMEM((8, 256, 256), BF16),
+        pltpu.VMEM((8, 128, 256), BF16),
+        pltpu.VMEM((GROUP, 8, 16, 256), BF16),
+        pltpu.VMEM((groups, 8, 16, 256), BF16),
+        pltpu.VMEM((8, 512, 256), BF16),
+        pltpu.VMEM((4, 8, width), F32),
+        pltpu.VMEM((experts + groups, 8, width), F32),
+        pltpu.SemaphoreType.DMA((8,)),
+        pltpu.SemaphoreType.DMA((14,)),
+        pltpu.SemaphoreType.DMA((semaphores,)),
+        pltpu.SemaphoreType.DMA((semaphores,)),
     ]
     return pl.pallas_call(
-        kernel,
-        in_specs=[hbm, hbm, vmem, smem, vmem, vmem, hbm, hbm, vmem, hbm],
-        out_specs=[hbm, hbm, hbm, hbm, hbm, vmem],
+        functools.partial(kernel, experts),
+        in_specs=[hbm, hbm, vmem, smem, vmem, vmem, hbm, hbm, vmem, hbm, hbm],
+        out_specs=[hbm] * 6 + [vmem] * 2,
         out_shape=[
             shape(tokens.shape, BF16),
             shape(tokens.shape, BF16),
-            shape(weights.shape, BF16),
+            shape(expert_in.shape, BF16),
+            shape(expert_out.shape, BF16),
             shape(wqkv.shape, BF16),
             shape(wattn.shape, BF16),
             shape((8, width), F32),
+            shape((1, 2), F32),
         ],
         scratch_shapes=scratch,
-        compiler_params=pltpu.CompilerParams(vmem_limit_bytes=60 * 1024 * 1024),
-    )(tokens, cotangent, segments, live, ln1, ln2, wqkv, wattn, logits, weights)
-
-
-def to_units(w_in, w_out):
-    return jnp.stack([w_in[:, :512], w_out[:512], w_in[:, 512:], w_out[512:]])
+        compiler_params=pltpu.CompilerParams(
+            vmem_limit_bytes=63 * 1024 * 1024, collective_id=0, has_side_effects=True
+        ),
+    )(tokens, cotangent, segments, live, ln1, ln2, wqkv, wattn, logits, expert_in, expert_out)
 
 
 def body(
     tokens, segment_ids, live_tokens, cotangent, ln1_gain, ln1_bias, qkv_weight, attn_weight,
     ln2_gain, ln2_bias, task_logits, expert_in, expert_out,
 ):
-    experts = lax.axis_size("expert")
-    flip = [(i, i ^ 1) for i in range(experts)]
-    up = [(i, (i + 2) % experts) for i in range(experts)]
-    down = [((i + 2) % experts, i) for i in range(experts)]
-    own = to_units(expert_in[0], expert_out[0])
-    following = lax.ppermute(own, "expert", down)
-    partner = lax.ppermute(own, "expert", flip)
-    following_partner = lax.ppermute(following, "expert", flip)
-    weights = jnp.stack([own, partner, following, following_partner])
     ln1 = jnp.stack([ln1_gain, ln1_bias]).astype(F32)
     ln2 = jnp.stack([ln2_gain, ln2_bias]).astype(F32)
-    out, grad_in, grads, qkv_grad, attn_grad, vectors = one_device(
-        tokens[0], cotangent[0], segment_ids, live_tokens, ln1, ln2, qkv_weight, attn_weight,
-        task_logits, weights,
+    out, grad_in, in_grad, out_grad, qkv_grad, attn_grad, vectors, logits_grad = one_device(
+        lax.axis_size("expert"), tokens[0], cotangent[0], segment_ids, live_tokens, ln1, ln2,
+        qkv_weight, attn_weight, task_logits, expert_in[0], expert_out[0],
     )
-    here = grads[0].astype(F32) + lax.ppermute(grads[1], "expert", flip).astype(F32)
-    there = grads[2].astype(F32) + lax.ppermute(grads[3], "expert", flip).astype(F32)
-    here = here + lax.ppermute(there.astype(BF16), "expert", up).astype(F32)
-    gate_grad = vectors[4, :2]
-    here, gate_grad = lax.psum((here, gate_grad), "dp")
-    gates = jax.nn.softmax(task_logits[0])
-    logits_grad = (gates * (gate_grad - jnp.sum(gates * gate_grad)))[None]
-    sums = lax.psum(
-        (vectors[:4], qkv_grad.astype(F32), attn_grad.astype(F32)), ("expert", "dp")
-    )
-    expert_in_grad = jnp.concatenate([here[0], here[2]], axis=1)[None]
-    expert_out_grad = jnp.concatenate([here[1], here[3]], axis=0)[None]
     return (
-        out[None], grad_in[None], sums[0][0], sums[0][1], sums[1], sums[2], sums[0][2], sums[0][3],
-        logits_grad, expert_in_grad, expert_out_grad,
+        out[None], grad_in[None], vectors[0], vectors[1], qkv_grad.astype(F32),
+        attn_grad.astype(F32), vectors[2], vectors[3], logits_grad,
+        in_grad.astype(F32)[None], out_grad.astype(F32)[None],
     )
 
 

time: 444 us -> 179 us (0.40)
  the two profiles are of different devices: /device:TPU:1 before, /device:TPU:11 now
where the time goes in v1:
time: 179 us
  Pallas kernels  163 us (91%)
  other arithmetic  8.48 us (5%)
  local copies, waits for them, and re-layouts  6.66 us (4%)
    pallas_call x1, Pallas kernels, one_device(): pl.pallas_call(functools.partial(kernel, experts), in_specs=[hbm, hbm, vm...  163 us
    convert_element_type x1, other arithmetic, body(): qkv_grad.astype(F32)  3.6 us

profile of v1, /device:TPU:11, one launch (start us, length us, event | category | flops | bytes accessed | tf_op | source)
XLA Modules:
  0.0 179.0 jit_solution(2341626551433206534)
XLA Ops:
  1.3 0.7 stack.19
  2.0 0.7 stack.18
  2.7 0.7 stack.22
  3.3 0.7 stack.21
  4.0 0.6 maximum_convert_fusion
  4.6 162.5 %shard_map.212 = (bf16[1024,512]{1,0:T(8,128)(2,1)}, bf16[1024,512]{1,0:T(8,128)(2,1)}, bf16[512,1024]{1,0:T(8,128)(2,1)}, bf16[1024,512]{1,0:T(8,128)(2,1)}, bf...) custom-call(bf16[1024,512]{1,0:T(8,128)(2,1)} %bitcast.18, ...), custom_call_target="tpu_custom_call" | custom-call | tf_op jit(solution)/shard_map/pallas_call | solution.py:791
  167.1 1.5 fusion
  168.6 0.0 copy-start.4
  168.6 0.0 copy-start.1
  168.6 3.6 %convert_element_type.16 = f32[512,1536]{1,0:T(8,128)} convert(bf16[512,1536]{1,0:T(8,128)(2,1)} %get-tuple-element.22) | non-fusion elementwise | flops 786432 | bytes 4718592 | tf_op jit(solution)/shard_map/convert_element_type | solution.py:823
  172.2 0.0 copy-done.4
  172.2 0.0 copy-start
  172.2 1.1 convert_element_type.17
  173.3 0.0 copy-done.1
  173.3 1.6 bitcast_convert_fusion.1
  174.9 0.0 copy-start.3
  174.9 0.0 copy-done
  174.9 0.0 copy-start.2
  174.9 1.6 bitcast_convert_fusion
  176.5 0.0 copy-done.3
  176.5 0.0 copy-start.5
  176.5 1.0 copy.28
  177.5 0.0 copy-done.2
  177.5 1.0 copy.29
  178.4 0.0 copy-done.5
  178.4 0.5 copy.30
Async XLA Ops:
  168.6 3.6 %copy-start.4 = (bf16[512,512]{1,0:T(8,128)(2,1)S(1)}, bf16[512,512]{1,0:T(8,128)(2,1)}, u32[]{:S(2)}) copy-start(bf16[512,512]{1,0:T(8,128)(2,1)} %get-tuple-element.23) | copy-start | bytes 1572868
  168.6 4.7 %copy-start.1 = (bf16[512,1024]{1,0:T(8,128)(2,1)S(1)}, bf16[512,1024]{1,0:T(8,128)(2,1)}, u32[]{:S(2)}) copy-start(bf16[512,1024]{1,0:T(8,128)(2,1)} %get-tuple-element.25) | copy-start | bytes 3145732
  172.2 2.7 %copy-start = (bf16[1024,512]{1,0:T(8,128)(2,1)S(1)}, bf16[1024,512]{1,0:T(8,128)(2,1)}, u32[]{:S(2)}) copy-start(bf16[1024,512]{1,0:T(8,128)(2,1)} %get-tuple-element.26) | copy-start | bytes 3145732
  174.9 1.6 copy-start.3
  174.9 2.6 %copy-start.2 = (bf16[1024,512]{1,0:T(8,128)(2,1)S(1)}, bf16[1024,512]{1,0:T(8,128)(2,1)}, u32[]{:S(2)}) copy-start(bf16[1024,512]{1,0:T(8,128)(2,1)} %get-tuple-element.20) | copy-start | bytes 3145732
  176.5 1.9 %copy-start.5 = (f32[1,2]{1,0:T(1,128)S(1)}, f32[1,2]{1,0:T(1,128)}, u32[]{:S(2)}) copy-start(f32[1,2]{1,0:T(1,128)} %get-tuple-element.52) | copy-start | bytes 28

commit v2 on v1

v2 whole, which is shorter than its diff:
```python
import functools

import jax
import jax.numpy as jnp
from jax import lax
from jax.experimental import pallas as pl
from jax.experimental.pallas import tpu as pltpu
from jax.sharding import PartitionSpec as P

F32 = jnp.float32
BF16 = jnp.bfloat16
HEAD_DIM = 64
NORM_EPS = 1e-05
MASKED = -1e30
LOG2E = 1.4426950408889634
GELU_A = 0.7978845608028654
GELU_B = 0.044715


def dot_nn(a, b):
    return jnp.dot(a, b, preferred_element_type=F32)


def dot_nt(a, b):
    return lax.dot_general(a, b, (((1,), (1,)), ((), ())), preferred_element_type=F32)


def dot_tn(a, b):
    return lax.dot_general(a, b, (((0,), (0,)), ((), ())), preferred_element_type=F32)


def dot_tt(a, b):
    return lax.dot_general(a, b, (((0,), (1,)), ((), ())), preferred_element_type=F32)


def norm_parts(inputs):
    row_mean = jnp.mean(inputs, axis=-1, keepdims=True)
    centred = inputs - row_mean
    variance = jnp.mean(centred * centred, axis=-1, keepdims=True)
    inverse = lax.rsqrt(variance + NORM_EPS)
    return centred * inverse, inverse


def norm_back(scaled, normal, inverse):
    return inverse * (
        scaled
        - jnp.mean(scaled, axis=-1, keepdims=True)
        - normal * jnp.mean(scaled * normal, axis=-1, keepdims=True)
    )


def split_three(value):
    high = value.astype(BF16)
    rest = value - high.astype(F32)
    middle = rest.astype(BF16)
    low = (rest - middle.astype(F32)).astype(BF16)
    return high.astype(F32), middle.astype(F32), low.astype(F32)


def scaled_queries(queries):
    scaled = queries.astype(F32) * (LOG2E * HEAD_DIM ** (-0.5))
    high = scaled.astype(BF16)
    return high, (scaled - high.astype(F32)).astype(BF16)


def mask_rows(segments, live, length):
    position = lax.broadcasted_iota(jnp.int32, (16, length), 1)
    row = lax.broadcasted_iota(jnp.int32, (16, length), 0)
    segment = jnp.broadcast_to(segments, (16, length))
    alive = position < live
    for_query = jnp.where(
        row < 8,
        jnp.where(segment != row, MASKED, 0.0),
        jnp.where((row == 8) & alive, MASKED, 0.0),
    )
    for_key = jnp.where(
        row < 8,
        jnp.where(segment == row, 1.0, 0.0),
        jnp.where((row == 8) & (~alive), 1.0, 0.0),
    )
    for_key_back = jnp.where((row >= 9) & (row < 12), 1.0, for_key)
    return for_query, for_key, for_key_back


def head_rows(head, part, width):
    return pl.ds(pl.multiple_of(part * width + head * HEAD_DIM, HEAD_DIM), HEAD_DIM)


def key_band(start, size, tile, length):
    low = max(0, (start - 511) // tile * tile)
    high = min(length, -(-(start + size + 511) // tile) * tile)
    return low, high


def attend_forward(head, qkv_t, ctx_t, lse, mask_q, alive_row, q_aug, k_aug, v_aug, tile):
    width, length = ctx_t.shape
    high, low = scaled_queries(qkv_t[head_rows(head, 0, width), :])
    q_aug[0:64, :] = high
    q_aug[64:128, :] = low
    q_aug[128:144, :] = mask_q[...]
    keys = qkv_t[head_rows(head, 1, width), :]
    k_aug[0:64, :] = keys
    k_aug[64:128, :] = keys
    v_aug[0:64, :] = qkv_t[head_rows(head, 2, width), :]
    for start in range(0, length, tile):
        at = pl.ds(start, tile)
        scores = dot_tn(k_aug[...], q_aug[:, at])
        top = jnp.max(scores, axis=0, keepdims=True)
        weights = jnp.exp2(scores - top).astype(BF16)
        summed = dot_nn(v_aug[...], weights)
        total = summed[64:65, :]
        context = summed[0:64, :] * (1.0 / total)
        own = v_aug[0:64, at].astype(F32)
        ctx_t[head_rows(head, 0, width), at] = jnp.where(
            alive_row[:, at] > 0, context, own
        ).astype(BF16)
        lse[head, :, at] = top + jnp.log(total) * LOG2E


def attend_backward(head, qkv_t, dctx_t, ctx_t, lse, mask_q, q_aug, k_aug, v_aug, d_aug, dk, dv, tile):
    width, length = ctx_t.shape
    scale = HEAD_DIM ** (-0.5)
    row = lax.broadcasted_iota(jnp.int32, (16, length), 0)
    high, low = scaled_queries(qkv_t[head_rows(head, 0, width), :])
    q_aug[0:64, :] = high
    q_aug[64:128, :] = low
    one, two, three = split_three(-lse[head])
    q_aug[128:144, :] = jnp.where(
        row == 9, one, jnp.where(row == 10, two, jnp.where(row == 11, three, mask_q[...].astype(F32)))
    ).astype(BF16)
    keys = qkv_t[head_rows(head, 1, width), :]
    k_aug[0:64, :] = keys
    k_aug[64:128, :] = keys
    v_aug[0:64, :] = qkv_t[head_rows(head, 2, width), :]
    grad = dctx_t[head_rows(head, 0, width), :]
    d_aug[0:64, :] = grad
    context = ctx_t[head_rows(head, 0, width), :].astype(F32)
    one, two, three = split_three(
        -jnp.sum(grad.astype(F32) * context, axis=0, keepdims=True)
    )
    d_aug[64:80, :] = jnp.where(
        row == 0, one, jnp.where(row == 1, two, jnp.where(row == 2, three, 0.0))
    ).astype(BF16)
    dk[...] = jnp.zeros(dk.shape, F32)
    dv[...] = jnp.zeros(dv.shape, F32)
    for start in range(0, length, tile):
        first, last = key_band(start, tile, tile, length)
        at, near = pl.ds(start, tile), pl.ds(first, last - first)
        weights = jnp.exp2(dot_tn(q_aug[:, at], k_aug[:, near]))
        dweights = dot_tn(d_aug[:, at], v_aug[:, near])
        dscores = (weights * dweights).astype(BF16)
        dv[:, near] += dot_nn(d_aug[0:64, at], weights.astype(BF16))
        dk[:, near] += dot_nn(qkv_t[head_rows(head, 0, width), at], dscores)
        qkv_t[head_rows(head, 0, width), at] = (
            dot_nt(k_aug[0:64, near], dscores) * scale
        ).astype(BF16)
    qkv_t[head_rows(head, 1, width), :] = (dk[...] * scale).astype(BF16)
    qkv_t[head_rows(head, 2, width), :] = dv[...].astype(BF16)


def gelu_parts(u):
    square = u * u
    bend = jnp.tanh(u * (GELU_A + (GELU_A * GELU_B) * square))
    half = 0.5 + 0.5 * bend
    slope = half + (0.5 * u) * (1.0 - bend * bend) * (GELU_A + (3.0 * GELU_A * GELU_B) * square)
    return u * half, slope


MESH = pl.DeviceIdType.MESH
GROUP = 8


class Numbers:
    def __init__(self):
        self.used = 0

    def take(self, count):
        first = self.used
        self.used += count
        return first


def number_copies(groups):
    numbers = Numbers()
    names = {}
    for name, count in [
        ("w1x", 2), ("w1y", 2), ("w1c", 1), ("w1d", 2), ("w2a", 2), ("w2b", 2), ("w2c", 1), ("w2d", 1),
        ("w3x", 2), ("w3y", 2), ("w3c", 1), ("w3d", 2), ("gc", 8), ("g1", 4), ("g3y", 2), ("g3x", 2),
        ("gzu", 2), ("gzm", 2), ("gyr", 2), ("gya", 2), ("gfa", 2), ("gfb", 2),
        ("vec_dp", 3), ("vec_ex", GROUP - 1), ("vec_far", groups - 1),
    ]:
        names[name] = numbers.take(count)
    for index in range(4):
        names["sum", index] = numbers.take(4 + 2 * (2 * GROUP - 1) + groups - 1)
    return names, numbers.used


ROUNDS = (896, 384, 384, 384)


def kernel(
    experts,
    tokens, cotangent, segments, live, ln1_gain, ln1_bias, ln2_gain, ln2_bias, wqkv_in, wattn_in, logits,
    expert_in, expert_out,
    out, grad_in, in_grad, out_grad, qkv_grad, attn_grad, vectors, logits_grad,
    x, dy, wqkv, wattn, w, a1, qkv_t, ctx_t, lse, mid, a2, dz, hid, dpre, total, da2,
    dctx_t, alive_row, mask_q, q_aug, k_aug, v_aug, d_aug, dk, dv, gate_sum,
    rc, r1, r3y, r3x, rz, ryr, fin, part, ac, ay, ae, across, done, vec_dp, vec_ex,
    load_sem, store_sem, send_sem, recv_sem,
):
    length, width = x.shape
    tile = 256
    groups = experts // GROUP
    names, _ = number_copies(groups)
    expert = lax.axis_index("expert")
    dp = lax.axis_index("dp")
    core, row_y = dp % 2, dp // 2
    dp_core = dp + 1 - 2 * core
    dp_y = (dp + 2) % 4
    place = expert % GROUP
    base = expert - place
    mate_core = (expert, dp_core)
    mate_y = (expert, dp_y)
    mate_x = (expert + 1 - 2 * (expert % 2), dp)
    above = ((expert + 2) % experts, dp)
    below = ((expert + experts - 2) % experts, dp)

    def copy(src, dst, index, device):
        return pltpu.make_async_remote_copy(
            src_ref=src, dst_ref=dst, send_sem=send_sem.at[index], recv_sem=recv_sem.at[index],
            device_id=device, device_id_type=MESH,
        )

    def peer(step):
        return (base + (place + step) % GROUP, dp)

    def peer_y(step):
        return (base + (place + step) % GROUP, dp_y)

    def far(step):
        return ((expert + GROUP * step) % experts, dp)

    barrier = pltpu.get_barrier_semaphore()
    others = [mate_core, mate_y, mate_x, above, below] + [far(step) for step in range(1, groups)]
    for other in others:
        pl.semaphore_signal(barrier, inc=1, device_id=other, device_id_type=MESH)

    loads = [
        pltpu.make_async_copy(src, dst, load_sem.at[i])
        for i, (src, dst) in enumerate(
            [
                (expert_in.at[:, pl.ds(0, 512)], w.at[0, 0]),
                (expert_out.at[pl.ds(0, 512), :], w.at[0, 1]),
                (expert_in.at[:, pl.ds(512, 512)], w.at[0, 2]),
                (expert_out.at[pl.ds(512, 512), :], w.at[0, 3]),
                (tokens, x),
                (wqkv_in, wqkv),
                (wattn_in, wattn),
                (cotangent, dy),
            ]
        )
    ]
    for load in loads:
        load.start()
    live_count = live[0]
    alive_row[...] = jnp.where(
        lax.broadcasted_iota(jnp.int32, (1, length), 1) < live_count, 1.0, 0.0
    )
    for_query, for_key, for_key_back = mask_rows(segments[...], live_count, length)
    mask_q[...] = for_query.astype(BF16)
    k_aug[128:144, :] = for_key.astype(BF16)
    v_aug[64:80, :] = jnp.where(
        lax.broadcasted_iota(jnp.int32, (16, length), 0) == 0, 1.0, 0.0
    ).astype(BF16)
    gain1, bias1, gain2, bias2 = (
        ref[...].astype(F32).reshape(1, width) for ref in (ln1_gain, ln1_bias, ln2_gain, ln2_bias)
    )
    exponent = jnp.exp(logits[...] - jnp.max(logits[...], axis=1, keepdims=True))
    gates = exponent / jnp.sum(exponent, axis=1, keepdims=True)

    def halves(name, slot, unit, to_slot, device):
        return [
            copy(
                w.at[slot, unit, pl.ds(256 * h, 256), :], w.at[to_slot, unit, pl.ds(256 * h, 256), :],
                names[name] + h, device,
            )
            for h in range(2)
        ]

    w1x = halves("w1x", 0, dp, 1, mate_x)
    w1y = halves("w1y", 1, dp, 1, mate_y)
    w1d = halves("w1d", 1, dp_y, 1, mate_core)
    w1c = copy(w.at[1, dp], w.at[1, dp], names["w1c"], mate_core)
    w2a = halves("w2a", 0, dp, 2, below)
    w2b = halves("w2b", 0, dp_y, 2, below)
    w2c = copy(w.at[2, dp], w.at[2, dp], names["w2c"], mate_core)
    w2d = copy(w.at[2, dp_y], w.at[2, dp_y], names["w2d"], mate_core)
    w3x = halves("w3x", 2, dp, 3, mate_x)
    w3y = halves("w3y", 3, dp, 3, mate_y)
    w3d = halves("w3d", 3, dp_y, 3, mate_core)
    w3c = copy(w.at[3, dp], w.at[3, dp], names["w3c"], mate_core)

    for load in loads[:4]:
        load.wait()
    pl.semaphore_wait(barrier, len(others))
    for h in range(2):
        w1x[h].start()
        w2a[h].start()
    for h in range(2):
        w2b[h].start()

    loads[4].wait()
    for start in range(0, length, tile):
        at = pl.ds(start, tile)
        normal, inverse = norm_parts(x[at, :].astype(F32))
        a1[at, :] = (normal * gain1 + bias1).astype(BF16)
    loads[5].wait()
    for start in range(0, 3 * width, 512):
        at = pl.ds(start, 512)
        qkv_t[at, :] = dot_tt(wqkv[:, at], a1[...]).astype(BF16)

    def forward_heads(pair, carry):
        @pl.when(pair == 2)
        def _():
            w1x[0].wait_recv()
            w1y[0].start()
            w2a[0].wait_recv()
            w3x[0].start()

        for head in range(2):
            attend_forward(
                2 * pair + head, qkv_t, ctx_t, lse, mask_q, alive_row, q_aug, k_aug, v_aug, length
            )
        return carry

    lax.fori_loop(0, width // HEAD_DIM // 2, forward_heads, 0)
    w1x[1].wait_recv()
    w1y[1].start()
    w1c.start()
    w2a[1].wait_recv()
    w3x[1].start()
    w2c.start()

    loads[6].wait()
    loads[7].wait()
    for start in range(0, length, tile):
        at = pl.ds(start, tile)
        middle = x[at, :].astype(F32) + dot_tn(ctx_t[:, at], wattn[...])
        mid[at, :] = middle
        total[at, :] = middle
        normal, inverse = norm_parts(middle)
        a2[at, :] = (normal * gain2 + bias2).astype(BF16)
        alive = start + lax.broadcasted_iota(jnp.int32, (tile, 1), 0) < live_count
        live_dy = jnp.where(alive, dy[at, :], jnp.zeros((), BF16))
        dy[at, :] = live_dy
        for k in range(2):
            dz[k, at, :] = (gates[:, k : k + 1] * live_dy.astype(F32)).astype(BF16)
    da2[...] = jnp.zeros(da2.shape, F32)
    gate_sum[...] = jnp.zeros(gate_sum.shape, F32)

    def add_into(target, *terms):
        value = target[...].astype(F32)
        for term in terms:
            value = value + term[...].astype(F32)
        target[...] = value.astype(BF16)

    own_rows = pl.ds(pl.multiple_of(256 * row_y, 256), 256)
    other_rows = pl.ds(pl.multiple_of(256 * (1 - row_y), 256), 256)

    def unit(slot, chunk, rows=pl.ds(0, 512)):
        return w.at[slot, 2 * chunk + core, rows, :]

    def gc(slot, chunk):
        return copy(
            w.at[slot, 2 * chunk + 1 - core], rc.at[slot, chunk], names["gc"] + 2 * slot + chunk, mate_core
        )

    def add_core(slot, chunk):
        gc(slot, chunk).wait_recv()
        add_into(unit(slot, chunk), rc.at[slot, chunk])

    def g1(chunk, h):
        rows = pl.ds(256 * h, 256)
        return copy(unit(1, chunk, rows), r1.at[chunk, rows, :], names["g1"] + 2 * chunk + h, mate_x)

    def final(chunk, rows):
        return fin.at[2 * chunk + core, rows, :]

    g3y = [copy(unit(3, k, other_rows), r3y.at[k], names["g3y"] + k, mate_y) for k in range(2)]
    g3x = [copy(unit(3, k, own_rows), r3x.at[k], names["g3x"] + k, mate_x) for k in range(2)]

    def gzu(chunk):
        return copy(unit(2, chunk, other_rows), rz.at[chunk, other_rows, :], names["gzu"] + chunk, above)

    gzm = [copy(unit(2, k, own_rows), rz.at[k, own_rows, :], names["gzm"] + k, above) for k in range(2)]
    gyr = [copy(unit(0, k, other_rows), ryr.at[k], names["gyr"] + k, mate_y) for k in range(2)]
    gya = [copy(final(k, own_rows), final(k, own_rows), names["gya"] + k, mate_y) for k in range(2)]
    gfa = [copy(final(k, own_rows), final(k, own_rows), names["gfa"] + k, mate_core) for k in range(2)]
    gfb = [copy(final(k, other_rows), final(k, other_rows), names["gfb"] + k, mate_core) for k in range(2)]

    def slot_pair(turn, carry):
        later = turn // 3
        slots = (2 * ((turn + 3) // 4) + (turn % 3) // 2, 1 + 2 * ((turn % 3) // 2) - later)
        flips = (later, (turn + 2) // 3)
        chunks = tuple(row_y + flip * (1 - 2 * row_y) for flip in flips)

        def part_of(index, at):
            slot, chunk = slots[index], chunks[index]
            k = slot // 2
            w_in, w_out = w.at[slot, 2 * chunk], w.at[slot, 2 * chunk + 1]
            hidden, slope = gelu_parts(dot_nn(a2[at, :], w_in[...]))
            hid[index, at, :] = hidden.astype(BF16)
            dhidden = dot_nt(dz[k, at, :], w_out[...])
            dpre[index, at, :] = (dhidden * slope).astype(BF16)
            gate_sum[k] += jnp.sum(hidden * dhidden, axis=0, keepdims=True)

        blocks = [pl.ds(start, 512) for start in range(0, length, 512)]

        @pl.when(turn == 1)
        def _():
            w1y[1].wait_recv()
            w1d[1].start()
            w2c.wait_recv()

        @pl.when(turn == 2)
        def _():
            w3c.wait_recv()
            w3y[0].wait_recv()
            w3d[0].start()

        @pl.when(turn == 3)
        def _():
            w2d.wait_recv()

        for at in blocks:
            part_of(0, at)

        @pl.when(turn == 0)
        def _():
            w3x[0].wait_recv()
            w3y[0].start()
            w1y[0].wait_recv()
            w1d[0].start()
            w1c.wait_recv()

        @pl.when(turn == 1)
        def _():
            w3x[1].wait_recv()
            w3y[1].start()
            w3c.start()
            for h in range(2):
                w2b[h].wait_recv()
            w2d.start()
            for h in range(2):
                w1d[h].wait_recv()

        @pl.when(turn == 2)
        def _():
            w3y[1].wait_recv()
            w3d[1].start()
            add_core(2, row_y)
            add_core(1, 1 - row_y)
            for h in range(2):
                g1(1 - row_y, h).start()
            gzu(row_y).start()
            for h in range(2):
                w3d[h].wait_recv()

        for at in blocks:
            part_of(1, at)
            value = total[at, :]
            back = da2[at, :]
            for index in range(2):
                slot, chunk = slots[index], chunks[index]
                gate = jnp.where(slot < 2, gates[:, 0:1], gates[:, 1:2])
                value = value + gate * dot_nn(hid[index, at, :], w[slot, 2 * chunk + 1])
                back = back + dot_nt(dpre[index, at, :], w[slot, 2 * chunk])
            total[at, :] = value
            da2[at, :] = back

        @pl.when(turn == 0)
        def _():
            for each in w1x + w2a + w1y + [w1c]:
                each.wait_send()

        @pl.when(turn == 1)
        def _():
            for each in w3x + w1d + [w2c]:
                each.wait_send()
            add_core(0, row_y)
            add_core(1, row_y)
            for h in range(2):
                g1(row_y, h).start()

        @pl.when(turn == 2)
        def _():
            for each in w3y + w3d + [w3c]:
                each.wait_send()

        @pl.when(turn == 3)
        def _():
            for each in w2b + [w2d]:
                each.wait_send()
            for k in range(2):
                add_core(3, k)
                g3y[k].start()

        for index in range(2):
            slot, chunk = slots[index], chunks[index]
            k = slot // 2
            w[slot, 2 * chunk] = dot_tn(a2[...], dpre[index]).astype(BF16)
            w[slot, 2 * chunk + 1] = dot_tn(hid[index], dz[k]).astype(BF16)
            gc(slot, chunk).start()
        return carry

    lax.fori_loop(0, 4, slot_pair, 0)

    gain_sum = jnp.zeros((1, width), F32)
    bias_sum = jnp.zeros((1, width), F32)
    for start in range(0, length, tile):
        at = pl.ds(start, tile)
        normal, inverse = norm_parts(mid[at, :])
        grad = da2[at, :]
        gain_sum += jnp.sum(grad * normal, axis=0, keepdims=True)
        bias_sum += jnp.sum(grad, axis=0, keepdims=True)
        dmid = dy[at, :].astype(F32) + norm_back(grad * gain2, normal, inverse)
        mid[at, :] = dmid
        a2[at, :] = dmid.astype(BF16)
    vectors[2:3, :] = gain_sum
    vectors[3:4, :] = bias_sum
    vectors[4:5, :] = gate_sum[0]
    vectors[5:6, :] = gate_sum[1]
    vectors[6:8, :] = jnp.zeros((2, width), F32)
    add_core(2, 1 - row_y)
    gzu(1 - row_y).start()
    add_core(0, 1 - row_y)
    dctx_t[...] = dot_nt(wattn[...], a2[...]).astype(BF16)

    def sum_round(index, flat):
        first = names["sum", index]
        columns = ROUNDS[index]
        mine, landed, by_y, pieces, cross, result = (
            ref[index] for ref in (part, ac, ay, ae, across, done)
        )
        own_half = pl.ds(pl.multiple_of(256 * core, 256), 256)
        other_half = pl.ds(pl.multiple_of(256 * (1 - core), 256), 256)
        corner = 256 * core + 128 * row_y
        own_quarter = pl.ds(pl.multiple_of(corner, 128), 128)
        other_quarter = pl.ds(pl.multiple_of(256 * core + 128 * (1 - row_y), 128), 128)

        def rows(step, beyond=False):
            start = 256 * core + 128 * (1 - row_y) if beyond else corner
            return pl.ds(pl.multiple_of(start + 16 * ((place + step) % GROUP), 16), 16)

        to_core = copy(mine.at[other_half, :], landed, first, mate_core)
        to_y = copy(mine.at[other_quarter, :], by_y, first + 1, mate_y)
        back_y = copy(result.at[own_quarter, :], result.at[own_quarter, :], first + 2, mate_y)
        back_core = copy(result.at[own_half, :], result.at[own_half, :], first + 3, mate_core)
        routes = [(s, rows(s), peer(s)) for s in range(1, GROUP)]
        if flat:
            routes += [(GROUP + s, rows(s, True), peer_y(s)) for s in range(GROUP)]
        spread = [copy(mine.at[at, :], pieces.at[s], first + 3 + s, to) for s, at, to in routes]
        gather = [
            copy(result.at[rows(0), :], result.at[rows(0), :], first + 2 + 2 * GROUP + s, to)
            for s, _, to in routes
        ]
        over = [
            copy(cross.at[0], cross.at[s], first + 1 + 4 * GROUP + s, far(s)) for s in range(1, groups)
        ]

        def begin():
            to_core.start()

        def step_y():
            to_core.wait_recv()
            add_into(mine.at[own_half, :], landed)
            if flat:
                for each in spread:
                    each.start()
            else:
                to_y.start()

        def step_spread():
            to_y.wait_recv()
            add_into(mine.at[own_quarter, :], by_y)
            for each in spread:
                each.start()

        def step_gather():
            for each in spread:
                each.wait_recv()
            value = mine[rows(0), :].astype(F32)
            for s, _, _ in routes:
                value = value + pieces[s].astype(F32)
            if groups > 1:
                cross[0] = value.astype(BF16)
                for each in over:
                    each.start()
                for each in over:
                    each.wait_recv()

                def add_group(group, value):
                    step = (expert // GROUP - group + groups) % groups
                    return value + cross[step].astype(F32)

                value = lax.fori_loop(0, groups, add_group, jnp.zeros(value.shape, F32))
            result[rows(0), :] = value.astype(BF16)
            for each in gather:
                each.start()

        def step_back_y():
            for each in gather:
                each.wait_recv()
            if flat:
                back_core.start()
            else:
                back_y.start()

        def step_back_core():
            back_y.wait_recv()
            back_core.start()

        def end():
            back_core.wait_recv()

        def finish():
            for each in [to_core, back_core] + ([] if flat else [to_y, back_y]) + spread + gather + over:
                each.wait_send()

        if flat:
            return [begin, step_y, step_gather, step_back_y, end, finish]
        return [begin, step_y, step_spread, step_gather, step_back_y, step_back_core, end, finish]

    rounds = [sum_round(index, index == 3) for index in range(4)]

    k_aug[128:144, :] = for_key_back.astype(BF16)
    v_aug[64:80, :] = jnp.where(
        lax.broadcasted_iota(jnp.int32, (16, length), 0) < 3, 1.0, 0.0
    ).astype(BF16)

    def qkv_columns(pair):
        target = part[pair]
        first = target.shape[1] - 384
        for index in range(3):
            at = pl.ds(index * width + 128 * pair, 128)
            target[:, pl.ds(first + 128 * index, 128)] = dot_tt(a1[...], qkv_t[at, :]).astype(BF16)

    def take_x(k):
        g3y[k].wait_recv()
        add_into(unit(3, k, own_rows), r3y.at[k])
        g3x[k].start()

    def take_z(k):
        g3x[k].wait_recv()
        add_into(unit(2, k, own_rows), r3x.at[k])
        gzm[k].start()

    def take_y(k):
        gzu(k).wait_recv()
        add_into(unit(0, k, other_rows), rz.at[k, other_rows, :])
        gyr[k].start()

    def take_final(k):
        gyr[k].wait_recv()
        gzm[k].wait_recv()
        value = unit(0, k, own_rows)[...].astype(F32) + rz[k, own_rows, :].astype(F32)
        final(k, own_rows)[...] = (value + ryr[k].astype(F32)).astype(BF16)
        gya[k].start()
        gfa[k].start()

    def take_last(k):
        gya[k].wait_recv()
        gfb[k].start()

    def backward_heads(pair, carry):
        @pl.when(pair == 1)
        def _():
            part[0][:, 0:512] = dot_nn(ctx_t[...], a2[...]).astype(BF16)
            qkv_columns(0)
            rounds[0][0]()
            take_x(0)
            for k in range(2):
                for h in range(2):
                    g1(k, h).wait_recv()
                add_into(unit(0, k), r1.at[k])

        @pl.when(pair == 2)
        def _():
            qkv_columns(1)
            rounds[1][0]()
            rounds[0][1]()
            take_x(1)
            for k in range(2):
                take_y(k)

        @pl.when(pair == 3)
        def _():
            qkv_columns(2)
            rounds[2][0]()
            rounds[1][1]()
            rounds[0][2]()
            take_z(0)

        for head in range(2):
            attend_backward(
                2 * pair + head, qkv_t, dctx_t, ctx_t, lse, mask_q, q_aug, k_aug, v_aug, d_aug,
                dk, dv, tile,
            )
        return carry

    lax.fori_loop(0, width // HEAD_DIM // 2, backward_heads, 0)
    qkv_columns(3)
    rounds[3][0]()
    rounds[2][1]()
    rounds[1][2]()
    rounds[0][3]()
    take_z(1)

    stores = []

    def store(src, dst):
        stores.append(pltpu.make_async_copy(src, dst, store_sem.at[len(stores)]))
        stores[-1].start()

    dz[0] = total[...].astype(BF16)
    store(dz.at[0], out)
    gain_sum = jnp.zeros((1, width), F32)
    bias_sum = jnp.zeros((1, width), F32)
    for start in range(0, length, tile):
        at = pl.ds(start, tile)
        grad = dot_tt(qkv_t[:, at], wqkv[...])
        normal, inverse = norm_parts(x[at, :].astype(F32))
        gain_sum += jnp.sum(grad * normal, axis=0, keepdims=True)
        bias_sum += jnp.sum(grad, axis=0, keepdims=True)
        a2[at, :] = (mid[at, :] + norm_back(grad * gain1, normal, inverse)).astype(BF16)
        if start == tile:
            rounds[3][1]()
            rounds[2][2]()
            rounds[1][3]()
            rounds[0][4]()
    store(a2, grad_in)
    vectors[0:1, :] = gain_sum
    vectors[1:2, :] = bias_sum

    vec_dp[dp] = vectors[...]
    to_dp = [
        copy(vec_dp.at[dp], vec_dp.at[dp], names["vec_dp"] + s - 1, (expert, (dp + s) % 4))
        for s in range(1, 4)
    ]
    for each in to_dp:
        each.start()
    take_final(0)
    rounds[2][3]()
    rounds[1][4]()
    rounds[0][5]()
    for each in to_dp:
        each.wait_recv()
    row_sum = vec_dp[0] + vec_dp[1] + vec_dp[2] + vec_dp[3]
    vec_ex[expert] = row_sum
    to_ex = [
        copy(vec_ex.at[expert], vec_ex.at[expert], names["vec_ex"] + s - 1, peer(s))
        for s in range(1, GROUP)
    ]
    for each in to_ex:
        each.start()
    scaled = jnp.sum(row_sum[4:6, :], axis=1, keepdims=True)
    pair_lane = lax.broadcasted_iota(jnp.int32, (1, 2), 1)
    scaled_pair = jnp.where(pair_lane == 0, scaled[0:1, :], scaled[1:2, :])
    logits_grad[...] = scaled_pair - gates * jnp.sum(scaled_pair, axis=1, keepdims=True)

    rounds[3][2]()
    take_final(1)
    rounds[2][4]()
    rounds[1][5]()
    rounds[0][6]()
    store(done[0].at[:, pl.ds(0, 512)], attn_grad)

    def store_columns(pair):
        first = ROUNDS[pair] - 384
        for index in range(3):
            store(
                done[pair].at[:, pl.ds(first + 128 * index, 128)],
                qkv_grad.at[:, pl.ds(index * width + 128 * pair, 128)],
            )

    store_columns(0)
    take_last(0)
    for each in to_ex:
        each.wait_recv()
    sums = [to_dp, to_ex]
    if groups > 1:
        vec_group = vec_ex[base]
        for s in range(1, GROUP):
            vec_group = vec_group + vec_ex[base + s]
        here = experts + expert // GROUP
        vec_ex[here] = vec_group
        to_far = [
            copy(vec_ex.at[here], vec_ex.at[here], names["vec_far"] + s - 1, far(s))
            for s in range(1, groups)
        ]
        for each in to_far:
            each.start()
        for each in to_far:
            each.wait_recv()
        sums.append(to_far)
        value = vec_ex[experts]
        for s in range(1, groups):
            value = value + vec_ex[experts + s]
    else:
        value = vec_ex[0]
        for s in range(1, GROUP):
            value = value + vec_ex[s]
    vectors[...] = value
    rounds[1][6]()
    store_columns(1)
    rounds[2][5]()
    rounds[3][3]()
    take_last(1)
    rounds[2][6]()
    store_columns(2)
    rounds[3][4]()
    store_columns(3)
    for each in gfa + gfb:
        each.wait_recv()
    for chunk in range(2):
        at = pl.ds(512 * chunk, 512)
        store(fin.at[2 * chunk], in_grad.at[:, at])
        store(fin.at[2 * chunk + 1], out_grad.at[at, :])
    for chunk in range(2):
        for slot in range(4):
            gc(slot, chunk).wait_send()
        gzu(chunk).wait_send()
        for h in range(2):
            g1(chunk, h).wait_send()
    for group in [g3y, g3x, gzm, gyr, gya, gfa, gfb] + sums:
        for each in group:
            each.wait_send()
    for steps in rounds:
        steps[-1]()
    for each in stores:
        each.wait()


def one_device(
    experts, tokens, cotangent, segments, live, ln1_gain, ln1_bias, ln2_gain, ln2_bias, wqkv, wattn,
    logits, expert_in, expert_out,
):
    length, width = tokens.shape
    groups = experts // GROUP
    _, semaphores = number_copies(groups)
    vmem = pl.BlockSpec(memory_space=pltpu.VMEM)
    smem = pl.BlockSpec(memory_space=pltpu.SMEM)
    hbm = pl.BlockSpec(memory_space=pl.ANY)
    shape = jax.ShapeDtypeStruct

    def by_round(*leading):
        return [pltpu.VMEM((*leading, columns), BF16) for columns in ROUNDS]

    scratch = [
        pltpu.VMEM((length, width), BF16),
        pltpu.VMEM((length, width), BF16),
        pltpu.VMEM(wqkv.shape, BF16),
        pltpu.VMEM(wattn.shape, BF16),
        pltpu.VMEM((4, 4, 512, 512), BF16),
        pltpu.VMEM((length, width), BF16),
        pltpu.VMEM((3 * width, length), BF16),
        pltpu.VMEM((width, length), BF16),
        pltpu.VMEM((width // HEAD_DIM, 1, length), F32),
        pltpu.VMEM((length, width), F32),
        pltpu.VMEM((length, width), BF16),
        pltpu.VMEM((2, length, width), BF16),
        pltpu.VMEM((2, length, 512), BF16),
        pltpu.VMEM((2, length, 512), BF16),
        pltpu.VMEM((length, width), F32),
        pltpu.VMEM((length, width), F32),
        pltpu.VMEM((width, length), BF16),
        pltpu.VMEM((1, length), F32),
        pltpu.VMEM((16, length), BF16),
        pltpu.VMEM((144, length), BF16),
        pltpu.VMEM((144, length), BF16),
        pltpu.VMEM((80, length), BF16),
        pltpu.VMEM((80, length), BF16),
        pltpu.VMEM((HEAD_DIM, length), F32),
        pltpu.VMEM((HEAD_DIM, length), F32),
        pltpu.VMEM((2, 1, 512), F32),
        pltpu.VMEM((4, 2, 512, 512), BF16),
        pltpu.VMEM((2, 512, 512), BF16),
        pltpu.VMEM((2, 256, 512), BF16),
        pltpu.VMEM((2, 256, 512), BF16),
        pltpu.VMEM((2, 512, 512), BF16),
        pltpu.VMEM((2, 256, 512), BF16),
        pltpu.VMEM((4, 512, 512), BF16),
        by_round(512),
        by_round(256),
        by_round(128),
        by_round(2 * GROUP, 16),
        by_round(groups, 16),
        by_round(512),
        pltpu.VMEM((4, 8, width), F32),
        pltpu.VMEM((experts + groups, 8, width), F32),
        pltpu.SemaphoreType.DMA((8,)),
        pltpu.SemaphoreType.DMA((19,)),
        pltpu.SemaphoreType.DMA((semaphores,)),
        pltpu.SemaphoreType.DMA((semaphores,)),
    ]
    return pl.pallas_call(
        functools.partial(kernel, experts),
        in_specs=[hbm, hbm, vmem, smem] + [vmem] * 4 + [hbm, hbm, vmem, hbm, hbm],
        out_specs=[hbm] * 6 + [vmem] * 2,
        out_shape=[
            shape(tokens.shape, BF16),
            shape(tokens.shape, BF16),
            shape(expert_in.shape, BF16),
            shape(expert_out.shape, BF16),
            shape(wqkv.shape, BF16),
            shape(wattn.shape, BF16),
            shape((8, width), F32),
            shape((1, 2), F32),
        ],
        scratch_shapes=scratch,
        compiler_params=pltpu.CompilerParams(
            vmem_limit_bytes=63 * 1024 * 1024, collective_id=0, has_side_effects=True
        ),
    )(
        tokens, cotangent, segments, live, ln1_gain, ln1_bias, ln2_gain, ln2_bias, wqkv, wattn, logits,
        expert_in, expert_out,
    )


def body(
    tokens, segment_ids, live_tokens, cotangent, ln1_gain, ln1_bias, qkv_weight, attn_weight,
    ln2_gain, ln2_bias, task_logits, expert_in, expert_out,
):
    out, grad_in, in_grad, out_grad, qkv_grad, attn_grad, vectors, logits_grad = one_device(
        lax.axis_size("expert"), tokens[0], cotangent[0], segment_ids, live_tokens, ln1_gain, ln1_bias,
        ln2_gain, ln2_bias, qkv_weight, attn_weight, task_logits, expert_in[0], expert_out[0],
    )
    return (
        out[None], grad_in[None], vectors[0], vectors[1], qkv_grad.astype(F32),
        attn_grad.astype(F32), vectors[2], vectors[3], logits_grad,
        in_grad.astype(F32)[None], out_grad.astype(F32)[None],
    )


def solution(mesh):
    rows = ("expert", "dp")
    in_specs = (
        P(rows, None, None), P(rows, None), P(rows), P(rows, None, None), P(), P(), P(), P(), P(), P(),
        P("expert", None), P("expert", None, None), P("expert", None, None),
    )
    out_specs = (
        P(rows, None, None), P(rows, None, None), P(), P(), P(), P(), P(), P(),
        P("expert", None), P("expert", None, None), P("expert", None, None),
    )
    return jax.shard_map(body, mesh=mesh, in_specs=in_specs, out_specs=out_specs, check_vma=False)
```

time: 179 us -> 155 us (0.87)
  the two profiles are of different devices: /device:TPU:11 before, /device:TPU:1 now
where the time goes in v2:
time: 155 us; the launch traced here: 153 us
  Pallas kernels  139 us (90%)
  other arithmetic  7.87 us (5%)
  local copies, waits for them, and re-layouts  3.94 us (3%)
    pallas_call x1, Pallas kernels, one_device(): pl.pallas_call(functools.partial(kernel, experts), in_specs=[hbm, hbm, vm...  139 us
    convert_element_type x1, other arithmetic, body(): qkv_grad.astype(F32)  3.6 us

profile of v2, /device:TPU:1, one launch (start us, length us, event | category | flops | bytes accessed | tf_op | source)
XLA Modules:
  0.0 152.6 jit_solution(18275992899656924154)
XLA Ops:
  1.3 139.5 %shard_map.212 = (bf16[1024,512]{1,0:T(8,128)(2,1)}, bf16[1024,512]{1,0:T(8,128)(2,1)}, bf16[512,1024]{1,0:T(8,128)(2,1)}, bf16[1024,512]{1,0:T(8,128)(2,1)}, bf...) custom-call(bf16[1024,512]{1,0:T(8,128)(2,1)} %bitcast.18, ...), custom_call_target="tpu_custom_call" | custom-call | tf_op jit(solution)/shard_map/pallas_call | solution.py:906
  140.8 1.5 fusion
  142.2 0.0 copy-start.4
  142.2 0.0 copy-start.1
  142.2 3.6 %convert_element_type.8 = f32[512,1536]{1,0:T(8,128)} convert(bf16[512,1536]{1,0:T(8,128)(2,1)} %get-tuple-element.22) | non-fusion elementwise | flops 786432 | bytes 4718592 | tf_op jit(solution)/shard_map/convert_element_type | solution.py:939
  145.8 0.0 copy-done.4
  145.8 0.0 copy-start
  145.8 1.1 convert_element_type.9
  146.9 0.0 copy-done.1
  146.9 1.6 %bitcast_convert_fusion.1 = f32[1,512,1024]{2,1,0:T(8,128)} fusion(bf16[512,1024]{1,0:T(8,128)(2,1)S(1)} %copy-done.1), kind=kLoop, calls=%fused_computation.1 | loop fusion | flops 524288 | bytes 3145728 | tf_op jit(solution)/shard_map/broadcast_in_dim | solution.py:941
  148.5 0.0 copy-start.3
  148.5 0.0 copy-done
  148.5 0.0 copy-start.2
  148.5 1.6 %bitcast_convert_fusion = f32[1,1024,512]{2,1,0:T(8,128)} fusion(bf16[1024,512]{1,0:T(8,128)(2,1)S(1)} %copy-done), kind=kLoop, calls=%fused_computation | loop fusion | flops 524288 | bytes 3145728 | tf_op jit(solution)/shard_map/broadcast_in_dim | solution.py:941
  150.1 0.0 copy-done.3
  150.1 0.0 copy-start.5
  150.1 1.0 copy.28
  151.1 0.0 copy-done.2
  151.1 1.0 copy.29
  152.1 0.0 copy-done.5
  152.1 0.5 copy.30
Async XLA Ops:
  142.2 3.6 %copy-start.4 = (bf16[512,512]{1,0:T(8,128)(2,1)S(1)}, bf16[512,512]{1,0:T(8,128)(2,1)}, u32[]{:S(2)}) copy-start(bf16[512,512]{1,0:T(8,128)(2,1)} %get-tuple-element.23) | copy-start | bytes 1572868
  142.2 4.7 %copy-start.1 = (bf16[512,1024]{1,0:T(8,128)(2,1)S(1)}, bf16[512,1024]{1,0:T(8,128)(2,1)}, u32[]{:S(2)}) copy-start(bf16[512,1024]{1,0:T(8,128)(2,1)} %get-tuple-element.25) | copy-start | bytes 3145732
  145.8 2.7 %copy-start = (bf16[1024,512]{1,0:T(8,128)(2,1)S(1)}, bf16[1024,512]{1,0:T(8,128)(2,1)}, u32[]{:S(2)}) copy-start(bf16[1024,512]{1,0:T(8,128)(2,1)} %get-tuple-element.26) | copy-start | bytes 3145732
  148.5 1.6 %copy-start.3 = (bf16[1024,512]{1,0:T(8,128)(2,1)S(1)}, bf16[1024,512]{1,0:T(8,128)(2,1)}, u32[]{:S(2)}) copy-start(bf16[1024,512]{1,0:T(8,128)(2,1)} %get-tuple-element.19) | copy-start | bytes 3145732
  148.5 2.6 %copy-start.2 = (bf16[1024,512]{1,0:T(8,128)(2,1)S(1)}, bf16[1024,512]{1,0:T(8,128)(2,1)}, u32[]{:S(2)}) copy-start(bf16[1024,512]{1,0:T(8,128)(2,1)} %get-tuple-element.20) | copy-start | bytes 3145732
  150.1 1.9 %copy-start.5 = (f32[1,2]{1,0:T(1,128)S(1)}, f32[1,2]{1,0:T(1,128)}, u32[]{:S(2)}) copy-start(f32[1,2]{1,0:T(1,128)} %get-tuple-element.50) | copy-start | bytes 28

commit v3 on v2

--- a/solution.py
+++ b/solution.py
@@ -1,4 +1,5 @@
 import functools
+import itertools
 
 import jax
 import jax.numpy as jnp
@@ -106,10 +107,9 @@
         at = pl.ds(start, tile)
         scores = dot_tn(k_aug[...], q_aug[:, at])
         top = jnp.max(scores, axis=0, keepdims=True)
-        weights = jnp.exp2(scores - top).astype(BF16)
-        summed = dot_nn(v_aug[...], weights)
-        total = summed[64:65, :]
-        context = summed[0:64, :] * (1.0 / total)
+        weights = jnp.exp2(scores - top)
+        total = jnp.sum(weights, axis=0, keepdims=True)
+        context = dot_nn(v_aug[0:64, :], (weights * (1.0 / total)).astype(BF16))
         own = v_aug[0:64, at].astype(F32)
         ctx_t[head_rows(head, 0, width), at] = jnp.where(
             alive_row[:, at] > 0, context, own
@@ -185,17 +185,64 @@
     names = {}
     for name, count in [
         ("w1x", 2), ("w1y", 2), ("w1c", 1), ("w1d", 2), ("w2a", 2), ("w2b", 2), ("w2c", 1), ("w2d", 1),
-        ("w3x", 2), ("w3y", 2), ("w3c", 1), ("w3d", 2), ("gc", 8), ("g1", 4), ("g3y", 2), ("g3x", 2),
-        ("gzu", 2), ("gzm", 2), ("gyr", 2), ("gya", 2), ("gfa", 2), ("gfb", 2),
+        ("w3x", 2), ("w3y", 2), ("w3c", 1), ("w3d", 2), ("gc", 8), ("g1", 4), ("g3y", 4), ("g3x", 4),
+        ("gzu", 2), ("gzm", 4), ("gyr", 2), ("gya", 4), ("gfa", 4), ("gfb", 4),
         ("vec_dp", 3), ("vec_ex", GROUP - 1), ("vec_far", groups - 1),
     ]:
         names[name] = numbers.take(count)
-    for index in range(4):
-        names["sum", index] = numbers.take(4 + 2 * (2 * GROUP - 1) + groups - 1)
+    for index, levels in enumerate(LEVELS):
+        copies = sum(len(level_steps(level)) for level in levels)
+        names["sum", index] = numbers.take(2 * copies + groups - 1)
     return names, numbers.used
 
 
-ROUNDS = (896, 384, 384, 384)
+ROUNDS = (512, 384, 384, 384, 384)
+LEVELS = (("c", "x", "yz"), ("c", "y", "x", "z"), ("c", "x", "yz"), ("c", "x", "yz"), ("c", "x", "yz"))
+ORDER = {
+    "h0": [("a", 0), ("p", "y"), ("y", "y"), ("x", 0), ("p", "n"), ("x", 1)],
+    "h1": [("a", 0), ("x", 2)],
+    "h2": [("a", 1), ("z", 0), ("x", 3)],
+    "h3": [("y", "n"), ("a", 1), ("z", 1)],
+    "h4": [("a", 2), ("a", 0)],
+    "h5": [("a", 2), ("z", 2)],
+    "h6": [("a", 3), ("z", 3), ("f", 0), ("f", 1)],
+    "h7": [("a", 3), ("a", 2), ("a", 1)],
+    "E": [("a", 4), ("a", 0), ("f", 2), ("l", 0)],
+    "L1": [("f", 3), ("a", 4), ("a", 3)],
+    "L2": [("a", 1), ("l", 1)],
+    "L3": [("a", 2)],
+    "L4": [("a", 0), ("a", 4)],
+    "tail": [
+        ("l", 2), ("a", 1), ("l", 3), ("a", 0), ("a", 3), ("a", 0), ("a", 2), ("a", 1),
+        ("a", 4), ("vex",), ("a", 3), ("a", 2), ("a", 1), ("a", 2), ("a", 4), ("a", 3),
+        ("a", 1), ("vend",), ("a", 3), ("a", 4), ("a", 1), ("a", 4),
+    ],
+}
+AXES = {"x": 2, "y": 2, "c": 2, "z": GROUP // 2}
+
+
+def level_steps(level):
+    ranges = [range(AXES[axis] if axis in level else 1) for axis in "xycz"]
+    return [steps for steps in itertools.product(*ranges) if any(steps)]
+
+
+def share(rows, axes, place):
+    start, first = 0, 0
+    count, lanes = rows, 512
+    if "x" in axes:
+        count = count // AXES["x"]
+        start = start + count * place[0]
+    if "z" in axes:
+        count = count // AXES["z"]
+        start = start + count * place[3]
+    if "c" in axes:
+        lanes = lanes // AXES["c"]
+        first = first + lanes * place[2]
+    if "y" in axes:
+        lanes = lanes // AXES["y"]
+        first = first + lanes * place[1]
+    rows_at = pl.ds(0, count) if isinstance(start, int) else pl.ds(pl.multiple_of(start, 16), count)
+    return rows_at, pl.ds(pl.multiple_of(first, 128), lanes)
 
 
 def kernel(
@@ -205,7 +252,7 @@
     out, grad_in, in_grad, out_grad, qkv_grad, attn_grad, vectors, logits_grad,
     x, dy, wqkv, wattn, w, a1, qkv_t, ctx_t, lse, mid, a2, dz, hid, dpre, total, da2,
     dctx_t, alive_row, mask_q, q_aug, k_aug, v_aug, d_aug, dk, dv, gate_sum,
-    rc, r1, r3y, r3x, rz, ryr, fin, part, ac, ay, ae, across, done, vec_dp, vec_ex,
+    rc, r1, r3y, r3x, rz, ryr, fin, part, landed, across, done, vec_dp, vec_ex,
     load_sem, store_sem, send_sem, recv_sem,
 ):
     length, width = x.shape
@@ -216,6 +263,7 @@
     dp = lax.axis_index("dp")
     core, row_y = dp % 2, dp // 2
     dp_core = dp + 1 - 2 * core
+    here = (expert % 2, row_y, core, expert % GROUP // 2)
     dp_y = (dp + 2) % 4
     place = expert % GROUP
     base = expert - place
@@ -233,9 +281,6 @@
 
     def peer(step):
         return (base + (place + step) % GROUP, dp)
-
-    def peer_y(step):
-        return (base + (place + step) % GROUP, dp_y)
 
     def far(step):
         return ((expert + GROUP * step) % experts, dp)
@@ -269,9 +314,6 @@
     for_query, for_key, for_key_back = mask_rows(segments[...], live_count, length)
     mask_q[...] = for_query.astype(BF16)
     k_aug[128:144, :] = for_key.astype(BF16)
-    v_aug[64:80, :] = jnp.where(
-        lax.broadcasted_iota(jnp.int32, (16, length), 0) == 0, 1.0, 0.0
-    ).astype(BF16)
     gain1, bias1, gain2, bias2 = (
         ref[...].astype(F32).reshape(1, width) for ref in (ln1_gain, ln1_bias, ln2_gain, ln2_bias)
     )
@@ -386,17 +428,39 @@
     def final(chunk, rows):
         return fin.at[2 * chunk + core, rows, :]
 
-    g3y = [copy(unit(3, k, other_rows), r3y.at[k], names["g3y"] + k, mate_y) for k in range(2)]
-    g3x = [copy(unit(3, k, own_rows), r3x.at[k], names["g3x"] + k, mate_x) for k in range(2)]
+    def quarter(own, h):
+        start = row_y if own else 1 - row_y
+        return pl.ds(pl.multiple_of(256 * start + 128 * h, 128), 128)
+
+    def pieces(name, device, src, dst):
+        return [
+            copy(src(k, h), dst(k, h), names[name] + 2 * k + h, device) for k in range(2) for h in range(2)
+        ]
+
+    def half_of(ref, k, h):
+        return ref.at[k, pl.ds(128 * h, 128), :]
+
+    g3y = pieces("g3y", mate_y, lambda k, h: unit(3, k, quarter(False, h)), functools.partial(half_of, r3y))
+    g3x = pieces("g3x", mate_x, lambda k, h: unit(3, k, quarter(True, h)), functools.partial(half_of, r3x))
+    gzm = pieces(
+        "gzm", above, lambda k, h: unit(2, k, quarter(True, h)), lambda k, h: rz.at[k, quarter(True, h), :]
+    )
 
     def gzu(chunk):
         return copy(unit(2, chunk, other_rows), rz.at[chunk, other_rows, :], names["gzu"] + chunk, above)
 
-    gzm = [copy(unit(2, k, own_rows), rz.at[k, own_rows, :], names["gzm"] + k, above) for k in range(2)]
-    gyr = [copy(unit(0, k, other_rows), ryr.at[k], names["gyr"] + k, mate_y) for k in range(2)]
-    gya = [copy(final(k, own_rows), final(k, own_rows), names["gya"] + k, mate_y) for k in range(2)]
-    gfa = [copy(final(k, own_rows), final(k, own_rows), names["gfa"] + k, mate_core) for k in range(2)]
-    gfb = [copy(final(k, other_rows), final(k, other_rows), names["gfb"] + k, mate_core) for k in range(2)]
+    def gyr(chunk):
+        return copy(unit(0, chunk, other_rows), ryr.at[chunk], names["gyr"] + chunk, mate_y)
+
+    def own_final(k, h):
+        return final(k, quarter(True, h))
+
+    def other_final(k, h):
+        return final(k, quarter(False, h))
+
+    gya = pieces("gya", mate_y, own_final, own_final)
+    gfa = pieces("gfa", mate_core, own_final, own_final)
+    gfb = pieces("gfb", mate_core, other_final, other_final)
 
     def slot_pair(turn, carry):
         later = turn // 3
@@ -412,7 +476,6 @@
             hid[index, at, :] = hidden.astype(BF16)
             dhidden = dot_nt(dz[k, at, :], w_out[...])
             dpre[index, at, :] = (dhidden * slope).astype(BF16)
-            gate_sum[k] += jnp.sum(hidden * dhidden, axis=0, keepdims=True)
 
         blocks = [pl.ds(start, 512) for start in range(0, length, 512)]
 
@@ -470,10 +533,13 @@
             part_of(1, at)
             value = total[at, :]
             back = da2[at, :]
+            live_dy = dy[at, :].astype(F32)
             for index in range(2):
                 slot, chunk = slots[index], chunks[index]
                 gate = jnp.where(slot < 2, gates[:, 0:1], gates[:, 1:2])
-                value = value + gate * dot_nn(hid[index, at, :], w[slot, 2 * chunk + 1])
+                branch = dot_nn(hid[index, at, :], w[slot, 2 * chunk + 1])
+                gate_sum[slot // 2] += jnp.sum(branch * live_dy, axis=0, keepdims=True)
+                value = value + gate * branch
                 back = back + dot_nt(dpre[index, at, :], w[slot, 2 * chunk])
             total[at, :] = value
             da2[at, :] = back
@@ -503,7 +569,8 @@
                 each.wait_send()
             for k in range(2):
                 add_core(3, k)
-                g3y[k].start()
+                for h in range(2):
+                    g3y[2 * k + h].start()
 
         for index in range(2):
             slot, chunk = slots[index], chunks[index]
@@ -536,185 +603,171 @@
     add_core(0, 1 - row_y)
     dctx_t[...] = dot_nt(wattn[...], a2[...]).astype(BF16)
 
-    def sum_round(index, flat):
-        first = names["sum", index]
-        columns = ROUNDS[index]
-        mine, landed, by_y, pieces, cross, result = (
-            ref[index] for ref in (part, ac, ay, ae, across, done)
-        )
-        own_half = pl.ds(pl.multiple_of(256 * core, 256), 256)
-        other_half = pl.ds(pl.multiple_of(256 * (1 - core), 256), 256)
-        corner = 256 * core + 128 * row_y
-        own_quarter = pl.ds(pl.multiple_of(corner, 128), 128)
-        other_quarter = pl.ds(pl.multiple_of(256 * core + 128 * (1 - row_y), 128), 128)
-
-        def rows(step, beyond=False):
-            start = 256 * core + 128 * (1 - row_y) if beyond else corner
-            return pl.ds(pl.multiple_of(start + 16 * ((place + step) % GROUP), 16), 16)
-
-        to_core = copy(mine.at[other_half, :], landed, first, mate_core)
-        to_y = copy(mine.at[other_quarter, :], by_y, first + 1, mate_y)
-        back_y = copy(result.at[own_quarter, :], result.at[own_quarter, :], first + 2, mate_y)
-        back_core = copy(result.at[own_half, :], result.at[own_half, :], first + 3, mate_core)
-        routes = [(s, rows(s), peer(s)) for s in range(1, GROUP)]
-        if flat:
-            routes += [(GROUP + s, rows(s, True), peer_y(s)) for s in range(GROUP)]
-        spread = [copy(mine.at[at, :], pieces.at[s], first + 3 + s, to) for s, at, to in routes]
-        gather = [
-            copy(result.at[rows(0), :], result.at[rows(0), :], first + 2 + 2 * GROUP + s, to)
-            for s, _, to in routes
-        ]
-        over = [
-            copy(cross.at[0], cross.at[s], first + 1 + 4 * GROUP + s, far(s)) for s in range(1, groups)
-        ]
+    def sum_round(index):
+        rows, levels = ROUNDS[index], LEVELS[index]
+        mine, cross, result = part[index], across[index], done[index]
+        number = names["sum", index]
+        scatter, gather, done_axes = [], [], []
+        axes = ""
+        for level, buffer in zip(levels, landed[index]):
+            axes = axes + level
+            done_axes.append(axes)
+            there, back = [], []
+            for slot, steps in enumerate(level_steps(level)):
+                x_there = here[0] + steps[0] * (1 - 2 * here[0])
+                y_there = here[1] + steps[1] * (1 - 2 * here[1])
+                c_there = here[2] + steps[2] * (1 - 2 * here[2])
+                z_there = (here[3] + steps[3]) % AXES["z"]
+                device = (base + 2 * z_there + x_there, 2 * y_there + c_there)
+                away = share(rows, axes, (x_there, y_there, c_there, z_there))
+                there.append(copy(mine.at[away], buffer.at[slot], number, device))
+                at = share(rows, axes, here)
+                back.append(copy(result.at[at], result.at[at], number + 1, device))
+                number += 2
+            scatter.append(there)
+            gather.append(back)
+        over = [copy(cross.at[0], cross.at[s], number + s - 1, far(s)) for s in range(1, groups)]
+        last = len(levels) - 1
+
+        def start_all(copies):
+            for each in copies:
+                each.start()
+
+        def wait_all(copies):
+            for each in copies:
+                each.wait_recv()
 
         def begin():
-            to_core.start()
-
-        def step_y():
-            to_core.wait_recv()
-            add_into(mine.at[own_half, :], landed)
-            if flat:
-                for each in spread:
-                    each.start()
-            else:
-                to_y.start()
-
-        def step_spread():
-            to_y.wait_recv()
-            add_into(mine.at[own_quarter, :], by_y)
-            for each in spread:
-                each.start()
-
-        def step_gather():
-            for each in spread:
-                each.wait_recv()
-            value = mine[rows(0), :].astype(F32)
-            for s, _, _ in routes:
-                value = value + pieces[s].astype(F32)
+            start_all(scatter[0])
+
+        def add_up(level):
+            wait_all(scatter[level])
+            at = share(rows, done_axes[level], here)
+            value = mine[at].astype(F32)
+            for slot in range(len(scatter[level])):
+                value = value + landed[index][level][slot].astype(F32)
+            if level < last:
+                mine[at] = value.astype(BF16)
+                start_all(scatter[level + 1])
+                return
             if groups > 1:
                 cross[0] = value.astype(BF16)
-                for each in over:
-                    each.start()
-                for each in over:
-                    each.wait_recv()
+                start_all(over)
+                wait_all(over)
 
                 def add_group(group, value):
                     step = (expert // GROUP - group + groups) % groups
                     return value + cross[step].astype(F32)
 
                 value = lax.fori_loop(0, groups, add_group, jnp.zeros(value.shape, F32))
-            result[rows(0), :] = value.astype(BF16)
-            for each in gather:
-                each.start()
-
-        def step_back_y():
-            for each in gather:
-                each.wait_recv()
-            if flat:
-                back_core.start()
+            result[at] = value.astype(BF16)
+            start_all(gather[last])
+
+        def pass_back(level):
+            wait_all(gather[level])
+            if level > 0:
+                start_all(gather[level - 1])
+
+        def finish():
+            for copies in scatter + gather + [over]:
+                for each in copies:
+                    each.wait_send()
+
+        steps = [begin] + [functools.partial(add_up, level) for level in range(last + 1)]
+        steps += [functools.partial(pass_back, level) for level in range(last, -1, -1)]
+        return steps, finish
+
+    rounds = [sum_round(index) for index in range(len(ROUNDS))]
+    progress = [0] * len(rounds)
+
+    def advance(index):
+        if progress[index] == 0 and index == 0:
+            part[0][...] = dot_nn(ctx_t[...], a2[...]).astype(BF16)
+        elif progress[index] == 0:
+            qkv_rows(index - 1)
+        rounds[index][0][progress[index]]()
+        progress[index] += 1
+        if progress[index] == len(rounds[index][0]):
+            if index == 0:
+                store(done[0], attn_grad)
             else:
-                back_y.start()
-
-        def step_back_core():
-            back_y.wait_recv()
-            back_core.start()
-
-        def end():
-            back_core.wait_recv()
-
-        def finish():
-            for each in [to_core, back_core] + ([] if flat else [to_y, back_y]) + spread + gather + over:
-                each.wait_send()
-
-        if flat:
-            return [begin, step_y, step_gather, step_back_y, end, finish]
-        return [begin, step_y, step_spread, step_gather, step_back_y, step_back_core, end, finish]
-
-    rounds = [sum_round(index, index == 3) for index in range(4)]
+                store_pair(index - 1)
 
     k_aug[128:144, :] = for_key_back.astype(BF16)
     v_aug[64:80, :] = jnp.where(
         lax.broadcasted_iota(jnp.int32, (16, length), 0) < 3, 1.0, 0.0
     ).astype(BF16)
 
-    def qkv_columns(pair):
-        target = part[pair]
-        first = target.shape[1] - 384
+    def qkv_rows(pair):
         for index in range(3):
             at = pl.ds(index * width + 128 * pair, 128)
-            target[:, pl.ds(first + 128 * index, 128)] = dot_tt(a1[...], qkv_t[at, :]).astype(BF16)
-
-    def take_x(k):
-        g3y[k].wait_recv()
-        add_into(unit(3, k, own_rows), r3y.at[k])
-        g3x[k].start()
-
-    def take_z(k):
-        g3x[k].wait_recv()
-        add_into(unit(2, k, own_rows), r3x.at[k])
-        gzm[k].start()
+            part[1 + pair][128 * index : 128 * index + 128, :] = dot_nn(qkv_t[at, :], a1[...]).astype(BF16)
+
+    def take_x(p):
+        g3y[p].wait_recv()
+        add_into(unit(3, p // 2, quarter(True, p % 2)), half_of(r3y, p // 2, p % 2))
+        g3x[p].start()
+
+    def take_z(p):
+        g3x[p].wait_recv()
+        add_into(unit(2, p // 2, quarter(True, p % 2)), half_of(r3x, p // 2, p % 2))
+        gzm[p].start()
+
+    def take_partner(k):
+        for h in range(2):
+            g1(k, h).wait_recv()
+        add_into(unit(0, k), r1.at[k])
 
     def take_y(k):
         gzu(k).wait_recv()
         add_into(unit(0, k, other_rows), rz.at[k, other_rows, :])
-        gyr[k].start()
-
-    def take_final(k):
-        gyr[k].wait_recv()
-        gzm[k].wait_recv()
-        value = unit(0, k, own_rows)[...].astype(F32) + rz[k, own_rows, :].astype(F32)
-        final(k, own_rows)[...] = (value + ryr[k].astype(F32)).astype(BF16)
-        gya[k].start()
-        gfa[k].start()
-
-    def take_last(k):
-        gya[k].wait_recv()
-        gfb[k].start()
-
-    def backward_heads(pair, carry):
-        @pl.when(pair == 1)
-        def _():
-            part[0][:, 0:512] = dot_nn(ctx_t[...], a2[...]).astype(BF16)
-            qkv_columns(0)
-            rounds[0][0]()
-            take_x(0)
-            for k in range(2):
-                for h in range(2):
-                    g1(k, h).wait_recv()
-                add_into(unit(0, k), r1.at[k])
-
-        @pl.when(pair == 2)
-        def _():
-            qkv_columns(1)
-            rounds[1][0]()
-            rounds[0][1]()
-            take_x(1)
-            for k in range(2):
-                take_y(k)
-
-        @pl.when(pair == 3)
-        def _():
-            qkv_columns(2)
-            rounds[2][0]()
-            rounds[1][1]()
-            rounds[0][2]()
-            take_z(0)
-
-        for head in range(2):
-            attend_backward(
-                2 * pair + head, qkv_t, dctx_t, ctx_t, lse, mask_q, q_aug, k_aug, v_aug, d_aug,
-                dk, dv, tile,
-            )
+        gyr(k).start()
+
+    def take_final(p):
+        k, h = p // 2, p % 2
+        if h == 0:
+            gyr(k).wait_recv()
+        gzm[p].wait_recv()
+        value = unit(0, k, quarter(True, h))[...].astype(F32) + rz[k, quarter(True, h), :].astype(F32)
+        own_final(k, h)[...] = (value + ryr[k, pl.ds(128 * h, 128), :].astype(F32)).astype(BF16)
+        gya[p].start()
+        gfa[p].start()
+
+    def take_last(p):
+        gya[p].wait_recv()
+        gfb[p].start()
+
+    def take(steps):
+        for name, *which in steps:
+            if name == "a":
+                advance(*which)
+            elif name == "x":
+                take_x(*which)
+            elif name == "z":
+                take_z(*which)
+            elif name == "p":
+                take_partner(row_y if which[0] == "y" else 1 - row_y)
+            elif name == "y":
+                take_y(row_y if which[0] == "y" else 1 - row_y)
+            elif name == "f":
+                take_final(*which)
+            elif name == "l":
+                take_last(*which)
+            elif name == "vex":
+                vectors_over_experts()
+            else:
+                vectors_end()
+
+    def backward_heads(head, carry):
+        for index in range(width // HEAD_DIM):
+            pl.when(head == index)(functools.partial(take, ORDER[f"h{index}"]))
+        attend_backward(
+            head, qkv_t, dctx_t, ctx_t, lse, mask_q, q_aug, k_aug, v_aug, d_aug, dk, dv, tile
+        )
         return carry
 
-    lax.fori_loop(0, width // HEAD_DIM // 2, backward_heads, 0)
-    qkv_columns(3)
-    rounds[3][0]()
-    rounds[2][1]()
-    rounds[1][2]()
-    rounds[0][3]()
-    take_z(1)
+    lax.fori_loop(0, width // HEAD_DIM, backward_heads, 0)
+    take(ORDER["E"])
 
     stores = []
 
@@ -726,18 +779,14 @@
     store(dz.at[0], out)
     gain_sum = jnp.zeros((1, width), F32)
     bias_sum = jnp.zeros((1, width), F32)
-    for start in range(0, length, tile):
+    for index, start in enumerate(range(0, length, tile)):
         at = pl.ds(start, tile)
         grad = dot_tt(qkv_t[:, at], wqkv[...])
         normal, inverse = norm_parts(x[at, :].astype(F32))
         gain_sum += jnp.sum(grad * normal, axis=0, keepdims=True)
         bias_sum += jnp.sum(grad, axis=0, keepdims=True)
         a2[at, :] = (mid[at, :] + norm_back(grad * gain1, normal, inverse)).astype(BF16)
-        if start == tile:
-            rounds[3][1]()
-            rounds[2][2]()
-            rounds[1][3]()
-            rounds[0][4]()
+        take(ORDER[f"L{index + 1}"])
     store(a2, grad_in)
     vectors[0:1, :] = gain_sum
     vectors[1:2, :] = bias_sum
@@ -749,77 +798,59 @@
     ]
     for each in to_dp:
         each.start()
-    take_final(0)
-    rounds[2][3]()
-    rounds[1][4]()
-    rounds[0][5]()
-    for each in to_dp:
-        each.wait_recv()
-    row_sum = vec_dp[0] + vec_dp[1] + vec_dp[2] + vec_dp[3]
-    vec_ex[expert] = row_sum
     to_ex = [
         copy(vec_ex.at[expert], vec_ex.at[expert], names["vec_ex"] + s - 1, peer(s))
         for s in range(1, GROUP)
     ]
-    for each in to_ex:
-        each.start()
-    scaled = jnp.sum(row_sum[4:6, :], axis=1, keepdims=True)
-    pair_lane = lax.broadcasted_iota(jnp.int32, (1, 2), 1)
-    scaled_pair = jnp.where(pair_lane == 0, scaled[0:1, :], scaled[1:2, :])
-    logits_grad[...] = scaled_pair - gates * jnp.sum(scaled_pair, axis=1, keepdims=True)
-
-    rounds[3][2]()
-    take_final(1)
-    rounds[2][4]()
-    rounds[1][5]()
-    rounds[0][6]()
-    store(done[0].at[:, pl.ds(0, 512)], attn_grad)
-
-    def store_columns(pair):
-        first = ROUNDS[pair] - 384
+    sums = [to_dp, to_ex]
+
+    def vectors_over_experts():
+        for each in to_dp:
+            each.wait_recv()
+        row_sum = vec_dp[0] + vec_dp[1] + vec_dp[2] + vec_dp[3]
+        vec_ex[expert] = row_sum
+        for each in to_ex:
+            each.start()
+        scaled = jnp.sum(row_sum[4:6, :], axis=1, keepdims=True)
+        pair_lane = lax.broadcasted_iota(jnp.int32, (1, 2), 1)
+        dgate = jnp.where(pair_lane == 0, scaled[0:1, :], scaled[1:2, :])
+        logits_grad[...] = gates * (dgate - jnp.sum(gates * dgate, axis=1, keepdims=True))
+
+    def vectors_end():
+        for each in to_ex:
+            each.wait_recv()
+        if groups > 1:
+            vec_group = vec_ex[base]
+            for s in range(1, GROUP):
+                vec_group = vec_group + vec_ex[base + s]
+            own = experts + expert // GROUP
+            vec_ex[own] = vec_group
+            to_far = [
+                copy(vec_ex.at[own], vec_ex.at[own], names["vec_far"] + s - 1, far(s))
+                for s in range(1, groups)
+            ]
+            for each in to_far:
+                each.start()
+            for each in to_far:
+                each.wait_recv()
+            sums.append(to_far)
+            value = vec_ex[experts]
+            for s in range(1, groups):
+                value = value + vec_ex[experts + s]
+        else:
+            value = vec_ex[0]
+            for s in range(1, GROUP):
+                value = value + vec_ex[s]
+        vectors[...] = value
+
+    def store_pair(pair):
         for index in range(3):
             store(
-                done[pair].at[:, pl.ds(first + 128 * index, 128)],
-                qkv_grad.at[:, pl.ds(index * width + 128 * pair, 128)],
+                done[1 + pair].at[pl.ds(128 * index, 128), :],
+                qkv_grad.at[pl.ds(index * width + 128 * pair, 128), :],
             )
 
-    store_columns(0)
-    take_last(0)
-    for each in to_ex:
-        each.wait_recv()
-    sums = [to_dp, to_ex]
-    if groups > 1:
-        vec_group = vec_ex[base]
-        for s in range(1, GROUP):
-            vec_group = vec_group + vec_ex[base + s]
-        here = experts + expert // GROUP
-        vec_ex[here] = vec_group
-        to_far = [
-            copy(vec_ex.at[here], vec_ex.at[here], names["vec_far"] + s - 1, far(s))
-            for s in range(1, groups)
-        ]
-        for each in to_far:
-            each.start()
-        for each in to_far:
-            each.wait_recv()
-        sums.append(to_far)
-        value = vec_ex[experts]
-        for s in range(1, groups):
-            value = value + vec_ex[experts + s]
-    else:
-        value = vec_ex[0]
-        for s in range(1, GROUP):
-            value = value + vec_ex[s]
-    vectors[...] = value
-    rounds[1][6]()
-    store_columns(1)
-    rounds[2][5]()
-    rounds[3][3]()
-    take_last(1)
-    rounds[2][6]()
-    store_columns(2)
-    rounds[3][4]()
-    store_columns(3)
+    take(ORDER["tail"])
     for each in gfa + gfb:
         each.wait_recv()
     for chunk in range(2):
@@ -830,15 +861,83 @@
         for slot in range(4):
             gc(slot, chunk).wait_send()
         gzu(chunk).wait_send()
+        gyr(chunk).wait_send()
         for h in range(2):
             g1(chunk, h).wait_send()
-    for group in [g3y, g3x, gzm, gyr, gya, gfa, gfb] + sums:
+    for group in [g3y, g3x, gzm, gya, gfa, gfb] + sums:
         for each in group:
             each.wait_send()
-    for steps in rounds:
-        steps[-1]()
+    for index, (steps, finish) in enumerate(rounds):
+        assert progress[index] == len(steps), (index, progress[index], len(steps))
+        finish()
     for each in stores:
         each.wait()
+
+
+def last_kernel(
+    out_low, grad_low, in_low, outg_low, qkv_low, attn_low, vectors,
+    out, grad_in, gain1, bias1, qkv_grad, attn_grad, gain2, bias2, in_grad, out_grad,
+    out_v, grad_v, in_v, outg_v, qkv_v, attn_v, in_f, outg_f, qkv_f, attn_f, load_sem, store_sem,
+):
+    loads = [
+        pltpu.make_async_copy(src, dst, load_sem.at[i])
+        for i, (src, dst) in enumerate(
+            [
+                (qkv_low, qkv_v), (in_low, in_v), (outg_low, outg_v), (attn_low, attn_v),
+                (out_low, out_v), (grad_low, grad_v),
+            ]
+        )
+    ]
+    for each in loads:
+        each.start()
+    for row, target in enumerate([gain1, bias1, gain2, bias2]):
+        target[...] = vectors[row : row + 1, :].reshape(target.shape)
+    width = attn_v.shape[0]
+    stores = []
+
+    def store(src, dst):
+        stores.append(pltpu.make_async_copy(src, dst, store_sem.at[len(stores)]))
+        stores[-1].start()
+
+    loads[0].wait()
+    for index in range(3):
+        at = pl.ds(index * width, width)
+        qkv_f[:, at] = qkv_v[at, :].astype(F32).T
+        store(qkv_f.at[:, at], qkv_grad.at[:, at])
+    for index, (low, wide, target) in enumerate(
+        [(in_v, in_f, in_grad), (outg_v, outg_f, out_grad), (attn_v, attn_f, attn_grad)]
+    ):
+        loads[1 + index].wait()
+        wide[...] = low[...].astype(F32)
+        store(wide, target)
+    for index, (low, target) in enumerate([(out_v, out), (grad_v, grad_in)]):
+        loads[4 + index].wait()
+        store(low, target)
+    for each in stores:
+        each.wait()
+
+
+def widen(out, grad_in, in_grad, out_grad, qkv_grad, attn_grad, vectors):
+    width = attn_grad.shape[0]
+    vmem = pl.BlockSpec(memory_space=pltpu.VMEM)
+    hbm = pl.BlockSpec(memory_space=pl.ANY)
+    shape = jax.ShapeDtypeStruct
+    low = [out.shape, grad_in.shape, in_grad.shape, out_grad.shape, qkv_grad.shape, attn_grad.shape]
+    wide = [in_grad.shape, out_grad.shape, (width, 3 * width), attn_grad.shape]
+    vector = shape((width,), F32)
+    return pl.pallas_call(
+        last_kernel,
+        in_specs=[hbm] * 6 + [vmem],
+        out_specs=[hbm] * 2 + [vmem] * 2 + [hbm] * 2 + [vmem] * 2 + [hbm] * 2,
+        out_shape=[
+            shape(out.shape, BF16), shape(grad_in.shape, BF16), vector, vector, shape(wide[2], F32),
+            shape(wide[3], F32), vector, vector, shape(wide[0], F32), shape(wide[1], F32),
+        ],
+        scratch_shapes=[pltpu.VMEM(each, BF16) for each in low]
+        + [pltpu.VMEM(each, F32) for each in wide]
+        + [pltpu.SemaphoreType.DMA((6,)), pltpu.SemaphoreType.DMA((8,))],
+        compiler_params=pltpu.CompilerParams(vmem_limit_bytes=63 * 1024 * 1024),
+    )(out, grad_in, in_grad, out_grad, qkv_grad, attn_grad, vectors)
 
 
 def one_device(
@@ -854,7 +953,19 @@
     shape = jax.ShapeDtypeStruct
 
     def by_round(*leading):
-        return [pltpu.VMEM((*leading, columns), BF16) for columns in ROUNDS]
+        return [pltpu.VMEM((*leading, rows, width), BF16) for rows in ROUNDS]
+
+    def level_buffers(rows, levels):
+        axes, buffers = "", []
+        for level in levels:
+            axes = axes + level
+            at, lanes = share(rows, axes, (0, 0, 0, 0))
+            buffers.append(pltpu.VMEM((len(level_steps(level)), at.size, lanes.size), BF16))
+        return buffers
+
+    def crossing(rows, levels):
+        at, lanes = share(rows, "".join(levels), (0, 0, 0, 0))
+        return pltpu.VMEM((groups, at.size, lanes.size), BF16)
 
     scratch = [
         pltpu.VMEM((length, width), BF16),
@@ -890,12 +1001,10 @@
         pltpu.VMEM((2, 512, 512), BF16),
         pltpu.VMEM((2, 256, 512), BF16),
         pltpu.VMEM((4, 512, 512), BF16),
-        by_round(512),
-        by_round(256),
-        by_round(128),
-        by_round(2 * GROUP, 16),
-        by_round(groups, 16),
-        by_round(512),
+        by_round(),
+        [level_buffers(rows, levels) for rows, levels in zip(ROUNDS, LEVELS)],
+        [crossing(rows, levels) for rows, levels in zip(ROUNDS, LEVELS)],
+        by_round(),
         pltpu.VMEM((4, 8, width), F32),
         pltpu.VMEM((experts + groups, 8, width), F32),
         pltpu.SemaphoreType.DMA((8,)),
@@ -912,7 +1021,7 @@
             shape(tokens.shape, BF16),
             shape(expert_in.shape, BF16),
             shape(expert_out.shape, BF16),
-            shape(wqkv.shape, BF16),
+            shape((3 * width, width), BF16),
             shape(wattn.shape, BF16),
             shape((8, width), F32),
             shape((1, 2), F32),
@@ -935,10 +1044,12 @@
         lax.axis_size("expert"), tokens[0], cotangent[0], segment_ids, live_tokens, ln1_gain, ln1_bias,
         ln2_gain, ln2_bias, qkv_weight, attn_weight, task_logits, expert_in[0], expert_out[0],
     )
+    (
+        out, grad_in, gain1, bias1, qkv_grad, attn_grad, gain2, bias2, in_grad, out_grad
+    ) = widen(out, grad_in, in_grad, out_grad, qkv_grad, attn_grad, vectors)
     return (
-        out[None], grad_in[None], vectors[0], vectors[1], qkv_grad.astype(F32),
-        attn_grad.astype(F32), vectors[2], vectors[3], logits_grad,
-        in_grad.astype(F32)[None], out_grad.astype(F32)[None],
+        out[None], grad_in[None], gain1, bias1, qkv_grad, attn_grad, gain2, bias2, logits_grad,
+        in_grad[None], out_grad[None],
     )
 
 

time: 155 us -> 130 us (0.84); the launches traced: 153 us -> 130 us
  Pallas kernels: 139 us -> 128 us
  other arithmetic: 7.87 us -> 0 us
  local copies, waits for them, and re-layouts: 3.94 us -> 0.52 us
    pallas_call x1, Pallas kernels: 139 us -> 121 us  [one_device(): pl.pallas_call(functools.partial(kernel, experts), in_specs=[hbm, hbm, vm...]
    pallas_call x0 -> x1, Pallas kernels: none -> 7.03 us  [widen(): pl.pallas_call(last_kernel, in_specs=[hbm] * 6 + [vmem], out_specs=[hbm]...]
    convert_element_type x2 -> x0, other arithmetic: 4.7 us -> none  [the longest x1 3.6 us: body(): qkv_grad.astype(F32)]
    broadcast_in_dim x2 -> x0, other arithmetic: 3.18 us -> none  [the longest x1 1.61 us: body(): out_grad.astype(F32)[None]]
    unnamed x15 -> x3, local copies, waits for them, and re-layouts: 2.47 us -> 0.52 us
where the time goes in v3:
time: 130 us
  Pallas kernels  128 us (98%)
  between operations  1.33 us (1%)
    pallas_call x1, Pallas kernels, one_device(): pl.pallas_call(functools.partial(kernel, experts), in_specs=[hbm, hbm, vm...  121 us
    pallas_call x1, Pallas kernels, widen(): pl.pallas_call(last_kernel, in_specs=[hbm] * 6 + [vmem], out_specs=[hbm]...  7.03 us

profile of v3, /device:TPU:1, one launch (start us, length us, event | category | flops | bytes accessed | tf_op | source)
XLA Modules:
  0.0 129.6 jit_solution(1021001326219074208)
XLA Ops:
  1.3 120.7 %shard_map.212 = (bf16[1024,512]{1,0:T(8,128)(2,1)}, bf16[1024,512]{1,0:T(8,128)(2,1)}, bf16[512,1024]{1,0:T(8,128)(2,1)}, bf16[1024,512]{1,0:T(8,128)(2,1)}, bf...) custom-call(bf16[1024,512]{1,0:T(8,128)(2,1)} %bitcast.8, ...), custom_call_target="tpu_custom_call" | custom-call | tf_op jit(solution)/shard_map/pallas_call | solution.py:1015
  122.0 0.0 copy-start
  122.0 7.0 %shard_map.213 = (bf16[1024,512]{1,0:T(8,128)(2,1)}, bf16[1024,512]{1,0:T(8,128)(2,1)}, f32[512]{0:T(512)}, f32[512]{0:T(512)}, f32[512,1536]{1,0:T(8,128)}, /*i...) custom-call(bf16[1024,512]{1,0:T(8,128)(2,1)} %get-tuple-element.29.out_low, ...), custom_call_target="tpu_custom_call" | custom-call | tf_op jit(solution)/shard_map/pallas_call | solution.py:928
  129.1 0.0 copy-done
  129.1 0.5 copy.26
Async XLA Ops:
  122.0 7.0 %copy-start = (f32[1,2]{1,0:T(1,128)S(1)}, f32[1,2]{1,0:T(1,128)}, u32[]{:S(2)}) copy-start(f32[1,2]{1,0:T(1,128)} %get-tuple-element.66) | copy-start | bytes 28

commit v4 on v3

--- a/solution.py
+++ b/solution.py
@@ -117,9 +117,8 @@
         lse[head, :, at] = top + jnp.log(total) * LOG2E
 
 
-def attend_backward(head, qkv_t, dctx_t, ctx_t, lse, mask_q, q_aug, k_aug, v_aug, d_aug, dk, dv, tile):
+def attend_backward_begin(head, qkv_t, dctx_t, ctx_t, lse, mask_q, q_aug, k_aug, v_aug, d_aug, dk, dv):
     width, length = ctx_t.shape
-    scale = HEAD_DIM ** (-0.5)
     row = lax.broadcasted_iota(jnp.int32, (16, length), 0)
     high, low = scaled_queries(qkv_t[head_rows(head, 0, width), :])
     q_aug[0:64, :] = high
@@ -143,18 +142,24 @@
     ).astype(BF16)
     dk[...] = jnp.zeros(dk.shape, F32)
     dv[...] = jnp.zeros(dv.shape, F32)
-    for start in range(0, length, tile):
-        first, last = key_band(start, tile, tile, length)
-        at, near = pl.ds(start, tile), pl.ds(first, last - first)
-        weights = jnp.exp2(dot_tn(q_aug[:, at], k_aug[:, near]))
-        dweights = dot_tn(d_aug[:, at], v_aug[:, near])
-        dscores = (weights * dweights).astype(BF16)
-        dv[:, near] += dot_nn(d_aug[0:64, at], weights.astype(BF16))
-        dk[:, near] += dot_nn(qkv_t[head_rows(head, 0, width), at], dscores)
-        qkv_t[head_rows(head, 0, width), at] = (
-            dot_nt(k_aug[0:64, near], dscores) * scale
-        ).astype(BF16)
-    qkv_t[head_rows(head, 1, width), :] = (dk[...] * scale).astype(BF16)
+
+
+def attend_backward_tile(head, qkv_t, q_aug, k_aug, v_aug, d_aug, dk, dv, start, tile):
+    length = qkv_t.shape[1]
+    queries = head_rows(head, 0, qkv_t.shape[0] // 3)
+    first, last = key_band(start, tile, tile, length)
+    at, near = pl.ds(start, tile), pl.ds(first, last - first)
+    weights = jnp.exp2(dot_tn(q_aug[:, at], k_aug[:, near]))
+    dweights = dot_tn(d_aug[:, at], v_aug[:, near])
+    dscores = (weights * dweights).astype(BF16)
+    dv[:, near] += dot_nn(d_aug[0:64, at], weights.astype(BF16))
+    dk[:, near] += dot_nn(qkv_t[queries, at], dscores)
+    qkv_t[queries, at] = (dot_nt(k_aug[0:64, near], dscores) * HEAD_DIM ** (-0.5)).astype(BF16)
+
+
+def attend_backward_end(head, qkv_t, dk, dv):
+    width = qkv_t.shape[0] // 3
+    qkv_t[head_rows(head, 1, width), :] = (dk[...] * HEAD_DIM ** (-0.5)).astype(BF16)
     qkv_t[head_rows(head, 2, width), :] = dv[...].astype(BF16)
 
 
@@ -197,25 +202,25 @@
 
 
 ROUNDS = (512, 384, 384, 384, 384)
-LEVELS = (("c", "x", "yz"), ("c", "y", "x", "z"), ("c", "x", "yz"), ("c", "x", "yz"), ("c", "x", "yz"))
+LEVELS = (("c", "x", "yz"), ("c", "y", "xz"), ("c", "x", "yz"), ("c", "y", "xz"), ("c", "x", "yz"))
 ORDER = {
-    "h0": [("a", 0), ("p", "y"), ("y", "y"), ("x", 0), ("p", "n"), ("x", 1)],
-    "h1": [("a", 0), ("x", 2)],
-    "h2": [("a", 1), ("z", 0), ("x", 3)],
-    "h3": [("y", "n"), ("a", 1), ("z", 1)],
-    "h4": [("a", 2), ("a", 0)],
-    "h5": [("a", 2), ("z", 2)],
-    "h6": [("a", 3), ("z", 3), ("f", 0), ("f", 1)],
-    "h7": [("a", 3), ("a", 2), ("a", 1)],
-    "E": [("a", 4), ("a", 0), ("f", 2), ("l", 0)],
-    "L1": [("f", 3), ("a", 4), ("a", 3)],
-    "L2": [("a", 1), ("l", 1)],
-    "L3": [("a", 2)],
-    "L4": [("a", 0), ("a", 4)],
+    "h0": [("a", 0, 0), ("p", "y"), ("y", "y"), ("x", 0), ("p", "n"), ("x", 1)],
+    "h1": [("a", 0, 1), ("x", 2)],
+    "h2": [("a", 1, 0), ("z", 0), ("x", 3), ("y", "n")],
+    "h3": [("a", 1, 1), ("z", 1)],
+    "h4": [("a", 2, 0), ("a", 0, 2)],
+    "h5": [("a", 2, 1), ("z", 2)],
+    "h6": [("a", 3, 0), ("z", 3), ("f", 0), ("f", 1)],
+    "h7": [("a", 1, 2), ("a", 3, 1), ("a", 2, 2)],
+    "E": [("a", 4, 0), ("a", 0, 3), ("f", 2), ("l", 0)],
+    "L1": [("f", 3), ("a", 4, 1)],
+    "L2": [("a", 1, 3), ("l", 1)],
+    "L3": [("a", 3, 2)],
+    "L4": [("a", 4, 2), ("a", 2, 3)],
     "tail": [
-        ("l", 2), ("a", 1), ("l", 3), ("a", 0), ("a", 3), ("a", 0), ("a", 2), ("a", 1),
-        ("a", 4), ("vex",), ("a", 3), ("a", 2), ("a", 1), ("a", 2), ("a", 4), ("a", 3),
-        ("a", 1), ("vend",), ("a", 3), ("a", 4), ("a", 1), ("a", 4),
+        ("a", 0, 4), ("a", 1, 4), ("l", 2), ("a", 3, 3), ("l", 3), ("a", 0, 5), ("a", 4, 3), ("a", 0, 6),
+        ("vex",), ("a", 2, 4), ("a", 1, 5), ("a", 3, 4), ("a", 1, 6), ("a", 4, 4), ("a", 2, 5), ("a", 3, 5),
+        ("a", 2, 6), ("vend",), ("a", 3, 6), ("a", 4, 5), ("a", 4, 6),
     ],
 }
 AXES = {"x": 2, "y": 2, "c": 2, "z": GROUP // 2}
@@ -247,12 +252,13 @@
 
 def kernel(
     experts,
-    tokens, cotangent, segments, live, ln1_gain, ln1_bias, ln2_gain, ln2_bias, wqkv_in, wattn_in, logits,
-    expert_in, expert_out,
-    out, grad_in, in_grad, out_grad, qkv_grad, attn_grad, vectors, logits_grad,
+    tokens, cotangent, segments_in, live, ln1_gain_in, ln1_bias_in, ln2_gain_in, ln2_bias_in, wqkv_in,
+    wattn_in, logits_in, expert_in, expert_out,
+    out, grad_in, in_grad, out_grad, qkv_grad, attn_grad, vectors_out, logits_grad_out,
+    segments, ln1_gain, ln1_bias, ln2_gain, ln2_bias, logits, vectors, logits_grad,
     x, dy, wqkv, wattn, w, a1, qkv_t, ctx_t, lse, mid, a2, dz, hid, dpre, total, da2,
     dctx_t, alive_row, mask_q, q_aug, k_aug, v_aug, d_aug, dk, dv, gate_sum,
-    rc, r1, r3y, r3x, rz, ryr, fin, part, landed, across, done, vec_dp, vec_ex,
+    rc, r1, r3y, r3x, rz, ryr, fin, part, landed, across, done, vec_dp, vec_ex, vec_sum,
     load_sem, store_sem, send_sem, recv_sem,
 ):
     length, width = x.shape
@@ -302,18 +308,27 @@
                 (wqkv_in, wqkv),
                 (wattn_in, wattn),
                 (cotangent, dy),
+                (segments_in, segments),
+                (ln1_gain_in, ln1_gain),
+                (ln1_bias_in, ln1_bias),
+                (ln2_gain_in, ln2_gain),
+                (ln2_bias_in, ln2_bias),
+                (logits_in, logits),
             ]
         )
     ]
-    for load in loads:
+    for load in loads[8:] + loads[4:5] + loads[:4] + loads[5:8]:
         load.start()
     live_count = live[0]
     alive_row[...] = jnp.where(
         lax.broadcasted_iota(jnp.int32, (1, length), 1) < live_count, 1.0, 0.0
     )
+    for load in loads[8:]:
+        load.wait()
     for_query, for_key, for_key_back = mask_rows(segments[...], live_count, length)
     mask_q[...] = for_query.astype(BF16)
-    k_aug[128:144, :] = for_key.astype(BF16)
+    for head in range(2):
+        k_aug[head, 128:144, :] = for_key.astype(BF16)
     gain1, bias1, gain2, bias2 = (
         ref[...].astype(F32).reshape(1, width) for ref in (ln1_gain, ln1_bias, ln2_gain, ln2_bias)
     )
@@ -342,6 +357,11 @@
     w3d = halves("w3d", 3, dp_y, 3, mate_core)
     w3c = copy(w.at[3, dp], w.at[3, dp], names["w3c"], mate_core)
 
+    loads[4].wait()
+    for start in range(0, length, tile):
+        at = pl.ds(start, tile)
+        normal, inverse = norm_parts(x[at, :].astype(F32))
+        a1[at, :] = (normal * gain1 + bias1).astype(BF16)
     for load in loads[:4]:
         load.wait()
     pl.semaphore_wait(barrier, len(others))
@@ -351,11 +371,6 @@
     for h in range(2):
         w2b[h].start()
 
-    loads[4].wait()
-    for start in range(0, length, tile):
-        at = pl.ds(start, tile)
-        normal, inverse = norm_parts(x[at, :].astype(F32))
-        a1[at, :] = (normal * gain1 + bias1).astype(BF16)
     loads[5].wait()
     for start in range(0, 3 * width, 512):
         at = pl.ds(start, 512)
@@ -371,7 +386,8 @@
 
         for head in range(2):
             attend_forward(
-                2 * pair + head, qkv_t, ctx_t, lse, mask_q, alive_row, q_aug, k_aug, v_aug, length
+                2 * pair + head, qkv_t, ctx_t, lse, mask_q, alive_row, q_aug.at[head], k_aug.at[head],
+                v_aug.at[head], length,
             )
         return carry
 
@@ -678,25 +694,23 @@
         return steps, finish
 
     rounds = [sum_round(index) for index in range(len(ROUNDS))]
-    progress = [0] * len(rounds)
-
-    def advance(index):
-        if progress[index] == 0 and index == 0:
+    def advance(index, step):
+        steps = rounds[index][0]
+        if step == 0 and index == 0:
             part[0][...] = dot_nn(ctx_t[...], a2[...]).astype(BF16)
-        elif progress[index] == 0:
+        elif step == 0:
             qkv_rows(index - 1)
-        rounds[index][0][progress[index]]()
-        progress[index] += 1
-        if progress[index] == len(rounds[index][0]):
-            if index == 0:
-                store(done[0], attn_grad)
-            else:
-                store_pair(index - 1)
-
-    k_aug[128:144, :] = for_key_back.astype(BF16)
-    v_aug[64:80, :] = jnp.where(
-        lax.broadcasted_iota(jnp.int32, (16, length), 0) < 3, 1.0, 0.0
-    ).astype(BF16)
+        steps[step]()
+        if step == len(steps) - 1 and index == 0:
+            store(done[0], attn_grad)
+        elif step == len(steps) - 1:
+            store_pair(index - 1)
+
+    for head in range(2):
+        k_aug[head, 128:144, :] = for_key_back.astype(BF16)
+        v_aug[head, 64:80, :] = jnp.where(
+            lax.broadcasted_iota(jnp.int32, (16, length), 0) < 3, 1.0, 0.0
+        ).astype(BF16)
 
     def qkv_rows(pair):
         for index in range(3):
@@ -758,15 +772,25 @@
             else:
                 vectors_end()
 
-    def backward_heads(head, carry):
-        for index in range(width // HEAD_DIM):
-            pl.when(head == index)(functools.partial(take, ORDER[f"h{index}"]))
-        attend_backward(
-            head, qkv_t, dctx_t, ctx_t, lse, mask_q, q_aug, k_aug, v_aug, d_aug, dk, dv, tile
-        )
+    def backward_heads(pair, carry):
+        def hook(part_of_pair):
+            for index in range(part_of_pair, width // HEAD_DIM, 2):
+                pl.when(2 * pair + part_of_pair == index)(functools.partial(take, ORDER[f"h{index}"]))
+
+        buffers = [[ref.at[head] for ref in (q_aug, k_aug, v_aug, d_aug, dk, dv)] for head in range(2)]
+        hook(0)
+        for head in range(2):
+            attend_backward_begin(2 * pair + head, qkv_t, dctx_t, ctx_t, lse, mask_q, *buffers[head])
+        for start in range(0, length, tile):
+            if start == length // 2:
+                hook(1)
+            for head in range(2):
+                attend_backward_tile(2 * pair + head, qkv_t, *buffers[head], start, tile)
+        for head in range(2):
+            attend_backward_end(2 * pair + head, qkv_t, dk.at[head], dv.at[head])
         return carry
 
-    lax.fori_loop(0, width // HEAD_DIM, backward_heads, 0)
+    lax.fori_loop(0, width // HEAD_DIM // 2, backward_heads, 0)
     take(ORDER["E"])
 
     stores = []
@@ -808,7 +832,7 @@
         for each in to_dp:
             each.wait_recv()
         row_sum = vec_dp[0] + vec_dp[1] + vec_dp[2] + vec_dp[3]
-        vec_ex[expert] = row_sum
+        vec_ex[expert] = row_sum[0:4, :]
         for each in to_ex:
             each.start()
         scaled = jnp.sum(row_sum[4:6, :], axis=1, keepdims=True)
@@ -841,7 +865,9 @@
             value = vec_ex[0]
             for s in range(1, GROUP):
                 value = value + vec_ex[s]
-        vectors[...] = value
+        vec_sum[...] = value
+        store(vec_sum, vectors_out)
+        store(logits_grad, logits_grad_out)
 
     def store_pair(pair):
         for index in range(3):
@@ -867,38 +893,42 @@
     for group in [g3y, g3x, gzm, gya, gfa, gfb] + sums:
         for each in group:
             each.wait_send()
-    for index, (steps, finish) in enumerate(rounds):
-        assert progress[index] == len(steps), (index, progress[index], len(steps))
+    for _, finish in rounds:
         finish()
     for each in stores:
         each.wait()
 
 
 def last_kernel(
-    out_low, grad_low, in_low, outg_low, qkv_low, attn_low, vectors,
-    out, grad_in, gain1, bias1, qkv_grad, attn_grad, gain2, bias2, in_grad, out_grad,
-    out_v, grad_v, in_v, outg_v, qkv_v, attn_v, in_f, outg_f, qkv_f, attn_f, load_sem, store_sem,
+    out_low, grad_low, in_low, outg_low, qkv_low, attn_low, vectors_in, logits_in,
+    out, grad_in, gain1, bias1, qkv_grad, attn_grad, gain2, bias2, logits_grad, in_grad, out_grad,
+    out_v, grad_v, in_v, outg_v, qkv_v, attn_v, vectors, logits_v, in_f, outg_f, qkv_f, attn_f, rows_f,
+    load_sem, store_sem,
 ):
     loads = [
         pltpu.make_async_copy(src, dst, load_sem.at[i])
         for i, (src, dst) in enumerate(
             [
                 (qkv_low, qkv_v), (in_low, in_v), (outg_low, outg_v), (attn_low, attn_v),
-                (out_low, out_v), (grad_low, grad_v),
+                (out_low, out_v), (grad_low, grad_v), (vectors_in, vectors), (logits_in, logits_v),
             ]
         )
     ]
-    for each in loads:
+    for each in loads[6:] + loads[:6]:
         each.start()
-    for row, target in enumerate([gain1, bias1, gain2, bias2]):
-        target[...] = vectors[row : row + 1, :].reshape(target.shape)
-    width = attn_v.shape[0]
     stores = []
 
     def store(src, dst):
         stores.append(pltpu.make_async_copy(src, dst, store_sem.at[len(stores)]))
         stores[-1].start()
 
+    loads[6].wait()
+    loads[7].wait()
+    for row, target in enumerate([gain1, bias1, gain2, bias2]):
+        rows_f[row][...] = vectors[row : row + 1, :].reshape(target.shape)
+        store(rows_f[row], target)
+    store(logits_v, logits_grad)
+    width = attn_v.shape[0]
     loads[0].wait()
     for index in range(3):
         at = pl.ds(index * width, width)
@@ -917,9 +947,8 @@
         each.wait()
 
 
-def widen(out, grad_in, in_grad, out_grad, qkv_grad, attn_grad, vectors):
+def widen(out, grad_in, in_grad, out_grad, qkv_grad, attn_grad, vectors, logits_grad):
     width = attn_grad.shape[0]
-    vmem = pl.BlockSpec(memory_space=pltpu.VMEM)
     hbm = pl.BlockSpec(memory_space=pl.ANY)
     shape = jax.ShapeDtypeStruct
     low = [out.shape, grad_in.shape, in_grad.shape, out_grad.shape, qkv_grad.shape, attn_grad.shape]
@@ -927,17 +956,20 @@
     vector = shape((width,), F32)
     return pl.pallas_call(
         last_kernel,
-        in_specs=[hbm] * 6 + [vmem],
-        out_specs=[hbm] * 2 + [vmem] * 2 + [hbm] * 2 + [vmem] * 2 + [hbm] * 2,
+        in_specs=[hbm] * 8,
+        out_specs=[hbm] * 11,
         out_shape=[
             shape(out.shape, BF16), shape(grad_in.shape, BF16), vector, vector, shape(wide[2], F32),
-            shape(wide[3], F32), vector, vector, shape(wide[0], F32), shape(wide[1], F32),
+            shape(wide[3], F32), vector, vector, shape(logits_grad.shape, F32), shape(wide[0], F32),
+            shape(wide[1], F32),
         ],
         scratch_shapes=[pltpu.VMEM(each, BF16) for each in low]
+        + [pltpu.VMEM(vectors.shape, F32), pltpu.VMEM(logits_grad.shape, F32)]
         + [pltpu.VMEM(each, F32) for each in wide]
-        + [pltpu.SemaphoreType.DMA((6,)), pltpu.SemaphoreType.DMA((8,))],
+        + [[pltpu.VMEM(vector.shape, F32) for _ in range(4)]]
+        + [pltpu.SemaphoreType.DMA((8,)), pltpu.SemaphoreType.DMA((13,))],
         compiler_params=pltpu.CompilerParams(vmem_limit_bytes=63 * 1024 * 1024),
-    )(out, grad_in, in_grad, out_grad, qkv_grad, attn_grad, vectors)
+    )(out, grad_in, in_grad, out_grad, qkv_grad, attn_grad, vectors, logits_grad)
 
 
 def one_device(
@@ -947,7 +979,6 @@
     length, width = tokens.shape
     groups = experts // GROUP
     _, semaphores = number_copies(groups)
-    vmem = pl.BlockSpec(memory_space=pltpu.VMEM)
     smem = pl.BlockSpec(memory_space=pltpu.SMEM)
     hbm = pl.BlockSpec(memory_space=pl.ANY)
     shape = jax.ShapeDtypeStruct
@@ -968,6 +999,14 @@
         return pltpu.VMEM((groups, at.size, lanes.size), BF16)
 
     scratch = [
+        pltpu.VMEM(segments.shape, jnp.int32),
+        pltpu.VMEM(ln1_gain.shape, BF16),
+        pltpu.VMEM(ln1_bias.shape, BF16),
+        pltpu.VMEM(ln2_gain.shape, BF16),
+        pltpu.VMEM(ln2_bias.shape, BF16),
+        pltpu.VMEM(logits.shape, F32),
+        pltpu.VMEM((8, width), F32),
+        pltpu.VMEM(logits.shape, F32),
         pltpu.VMEM((length, width), BF16),
         pltpu.VMEM((length, width), BF16),
         pltpu.VMEM(wqkv.shape, BF16),
@@ -987,12 +1026,12 @@
         pltpu.VMEM((width, length), BF16),
         pltpu.VMEM((1, length), F32),
         pltpu.VMEM((16, length), BF16),
-        pltpu.VMEM((144, length), BF16),
-        pltpu.VMEM((144, length), BF16),
-        pltpu.VMEM((80, length), BF16),
-        pltpu.VMEM((80, length), BF16),
-        pltpu.VMEM((HEAD_DIM, length), F32),
-        pltpu.VMEM((HEAD_DIM, length), F32),
+        pltpu.VMEM((2, 144, length), BF16),
+        pltpu.VMEM((2, 144, length), BF16),
+        pltpu.VMEM((2, 80, length), BF16),
+        pltpu.VMEM((2, 80, length), BF16),
+        pltpu.VMEM((2, HEAD_DIM, length), F32),
+        pltpu.VMEM((2, HEAD_DIM, length), F32),
         pltpu.VMEM((2, 1, 512), F32),
         pltpu.VMEM((4, 2, 512, 512), BF16),
         pltpu.VMEM((2, 512, 512), BF16),
@@ -1006,16 +1045,17 @@
         [crossing(rows, levels) for rows, levels in zip(ROUNDS, LEVELS)],
         by_round(),
         pltpu.VMEM((4, 8, width), F32),
-        pltpu.VMEM((experts + groups, 8, width), F32),
-        pltpu.SemaphoreType.DMA((8,)),
-        pltpu.SemaphoreType.DMA((19,)),
+        pltpu.VMEM((experts + groups, 4, width), F32),
+        pltpu.VMEM((4, width), F32),
+        pltpu.SemaphoreType.DMA((14,)),
+        pltpu.SemaphoreType.DMA((21,)),
         pltpu.SemaphoreType.DMA((semaphores,)),
         pltpu.SemaphoreType.DMA((semaphores,)),
     ]
     return pl.pallas_call(
         functools.partial(kernel, experts),
-        in_specs=[hbm, hbm, vmem, smem] + [vmem] * 4 + [hbm, hbm, vmem, hbm, hbm],
-        out_specs=[hbm] * 6 + [vmem] * 2,
+        in_specs=[hbm] * 3 + [smem] + [hbm] * 9,
+        out_specs=[hbm] * 8,
         out_shape=[
             shape(tokens.shape, BF16),
             shape(tokens.shape, BF16),
@@ -1023,7 +1063,7 @@
             shape(expert_out.shape, BF16),
             shape((3 * width, width), BF16),
             shape(wattn.shape, BF16),
-            shape((8, width), F32),
+            shape((4, width), F32),
             shape((1, 2), F32),
         ],
         scratch_shapes=scratch,
@@ -1045,8 +1085,8 @@
         ln2_gain, ln2_bias, qkv_weight, attn_weight, task_logits, expert_in[0], expert_out[0],
     )
     (
-        out, grad_in, gain1, bias1, qkv_grad, attn_grad, gain2, bias2, in_grad, out_grad
-    ) = widen(out, grad_in, in_grad, out_grad, qkv_grad, attn_grad, vectors)
+        out, grad_in, gain1, bias1, qkv_grad, attn_grad, gain2, bias2, logits_grad, in_grad, out_grad
+    ) = widen(out, grad_in, in_grad, out_grad, qkv_grad, attn_grad, vectors, logits_grad)
     return (
         out[None], grad_in[None], gain1, bias1, qkv_grad, attn_grad, gain2, bias2, logits_grad,
         in_grad[None], out_grad[None],

time: 130 us -> 125 us (0.962)
  Pallas kernels: 128 us -> 124 us
    pallas_call x2, Pallas kernels: 128 us -> 124 us  [the longest x1 118 us: one_device(): pl.pallas_call(functools.partial(kernel, experts), in_specs=[hbm] * 3 + [...]
where the time goes in v4:
time: 125 us
  Pallas kernels  124 us (99%)
  between operations  1.5 us (1%)
    pallas_call x1, Pallas kernels, one_device(): pl.pallas_call(functools.partial(kernel, experts), in_specs=[hbm] * 3 + [...  118 us
    pallas_call x1, Pallas kernels, widen(): pl.pallas_call(last_kernel, in_specs=[hbm] * 8, out_specs=[hbm] * 11, out...  5.81 us

profile of v4, /device:TPU:1, one launch (start us, length us, event | category | flops | bytes accessed | tf_op | source)
XLA Modules:
  0.0 125.1 jit_solution(14423132282539359957)
XLA Ops:
  1.3 117.8 %shard_map.212 = (bf16[1024,512]{1,0:T(8,128)(2,1)}, bf16[1024,512]{1,0:T(8,128)(2,1)}, bf16[512,1024]{1,0:T(8,128)(2,1)}, bf16[1024,512]{1,0:T(8,128)(2,1)}, bf...) custom-call(bf16[1024,512]{1,0:T(8,128)(2,1)} %bitcast.8, ...), custom_call_target="tpu_custom_call" | custom-call | tf_op jit(solution)/shard_map/pallas_call | solution.py:1055
  119.1 5.8 %shard_map.213 = (bf16[1024,512]{1,0:T(8,128)(2,1)}, bf16[1024,512]{1,0:T(8,128)(2,1)}, f32[512]{0:T(512)}, f32[512]{0:T(512)}, f32[512,1536]{1,0:T(8,128)}, /*i...) custom-call(bf16[1024,512]{1,0:T(8,128)(2,1)} %get-tuple-element.30., ...), custom_call_target="tpu_custom_call" | custom-call | tf_op jit(solution)/shard_map/pallas_call | solution.py:957

commit v5 on v4

--- a/solution.py
+++ b/solution.py
@@ -493,7 +493,7 @@
             dhidden = dot_nt(dz[k, at, :], w_out[...])
             dpre[index, at, :] = (dhidden * slope).astype(BF16)
 
-        blocks = [pl.ds(start, 512) for start in range(0, length, 512)]
+        blocks = [pl.ds(start, 256) for start in range(0, length, 256)]
 
         @pl.when(turn == 1)
         def _():

time: 125 us -> 125 us (level)
  no operation moved by 1% of the time
where the time goes in v5:
time: 125 us; the launch traced here: 124 us
  Pallas kernels  123 us (98%)
  between operations  1.5 us (1%)
    pallas_call x1, Pallas kernels, one_device(): pl.pallas_call(functools.partial(kernel, experts), in_specs=[hbm] * 3 + [...  117 us
    pallas_call x1, Pallas kernels, widen(): pl.pallas_call(last_kernel, in_specs=[hbm] * 8, out_specs=[hbm] * 11, out...  5.81 us

profile of v5, /device:TPU:1, one launch (start us, length us, event | category | flops | bytes accessed | tf_op | source)
XLA Modules:
  0.0 124.3 jit_solution(13869169379000666247)
XLA Ops:
  1.3 117.0 %shard_map.212 = (bf16[1024,512]{1,0:T(8,128)(2,1)}, bf16[1024,512]{1,0:T(8,128)(2,1)}, bf16[512,1024]{1,0:T(8,128)(2,1)}, bf16[1024,512]{1,0:T(8,128)(2,1)}, bf...) custom-call(bf16[1024,512]{1,0:T(8,128)(2,1)} %bitcast.8, ...), custom_call_target="tpu_custom_call" | custom-call | tf_op jit(solution)/shard_map/pallas_call | solution.py:1055
  118.3 5.8 %shard_map.213 = (bf16[1024,512]{1,0:T(8,128)(2,1)}, bf16[1024,512]{1,0:T(8,128)(2,1)}, f32[512]{0:T(512)}, f32[512]{0:T(512)}, f32[512,1536]{1,0:T(8,128)}, /*i...) custom-call(bf16[1024,512]{1,0:T(8,128)(2,1)} %get-tuple-element.30., ...), custom_call_target="tpu_custom_call" | custom-call | tf_op jit(solution)/shard_map/pallas_call | solution.py:957
